TPU v7x, 256 devices: a whole 4x4x8 slice. The times are simulated.
256 devices in a mesh: slab: 32 (over z_lo, y, core), tm: 8 (over x, z_hi).
Axes of the slice: x: 4, y: 4, z: 8 (z_hi: 2, z_lo: 4; z = z_hi * 4 + z_lo), core: 2. Of those that a mesh axis runs over, the one named last changes fastest.
Arguments:
- recording: bfloat16 [512, 65536], P('tm', 'slab'), may hold values from -6 to 6
- footprints: bfloat16 [2176, 8192], P(None, 'slab'), may hold values from -0.125 to 0.125
- traces: float32 [512, 8192], P('tm', 'slab'), may hold values from 0 to 2
- live_count: int32 [32], replicated, may hold values from 1 to 256, 6144 in all
Outputs:
- new_traces: float32 [512, 8192], P('tm', 'slab')
- new_footprints: bfloat16 [2176, 8192], P('tm', 'slab')
Inputs may be any that keep to these rules, and one draw needn't show every extreme that they name: Slots 0 .. live_count[s] - 1 of slab s are live; some slab has all 256 live.
All inputs are finite; a program needn't handle non-finite values.
Results may differ from a plain program's by a relative error of at most 0.0034.
Values may be sent and summed in bfloat16 or wider, within the bound.
A program may use at most 64 MiB of HBM per device.

v0:
```python
import jax
import jax.numpy as jnp
from jax import lax
from jax.sharding import PartitionSpec as P

GROUP = 128
GROUPS_DEV = 2


def passed_along(block, axis, distance):
    devices = range(lax.axis_size(axis))
    route = [(i - distance, i) for i in devices if i - distance in devices]
    return lax.ppermute(block, axis, route)


def with_halo(cells, sides, width):
    for axis, dim in sides:
        count = lax.axis_size(axis)
        ends = count - 1
        head = lax.slice_in_dim(cells, 0, width, axis=dim)
        tail = lax.slice_in_dim(cells, cells.shape[dim] - width, cells.shape[dim], axis=dim)
        cells = jnp.concatenate(
            [
                lax.ppermute(tail, axis, [(i, (i + 1) % count) for i in range(ends)]),
                cells,
                lax.ppermute(head, axis, [((i + 1) % count, i) for i in range(ends)]),
            ],
            axis=dim,
        )
    return cells


def contract_first(left, right):
    return lax.dot_general(
        left, right, (((0,), (0,)), ((), ())), preferred_element_type=jnp.float32
    )


def on_device(recording, footprints, traces, live_count):
    slabs = lax.axis_size("slab")
    slab_index = lax.axis_index("slab")
    neurons = traces.shape[1]
    extended = footprints.shape[0]
    voxels = recording.shape[1]
    rim_rows = extended - voxels
    slots = jnp.arange(neurons, dtype=jnp.int32)
    live_here = jnp.sum(jnp.where(jnp.arange(slabs, dtype=jnp.int32) == slab_index, live_count, 0))
    living = slots < live_here
    row_ids = jnp.arange(extended, dtype=jnp.int32)
    kept_mask = living[None, :] & ((row_ids[:, None] < voxels) | (slab_index < slabs - 1))
    masked_foot = jnp.where(kept_mask, footprints, jnp.zeros_like(footprints))
    start_tr = jnp.where(living[None, :], traces, jnp.zeros_like(traces))
    next_edge, movie_rim = passed_along(
        (masked_foot[:rim_rows], recording[:, :rim_rows]), "slab", -1
    )
    prev_rim = passed_along(masked_foot[voxels:], "slab", 1)
    movie_ext = jnp.concatenate([recording, movie_rim], 1)
    drive = jnp.dot(movie_ext, masked_foot, preferred_element_type=jnp.float32)
    gram_own = contract_first(masked_foot, masked_foot)
    gram_prev = contract_first(masked_foot[:rim_rows], prev_rim)
    gram_next = contract_first(masked_foot[voxels:], next_edge)
    diag_own = jnp.diagonal(gram_own) + 1e-06
    halo_tr = with_halo(start_tr, (("slab", 1),), neurons)
    prev_c = halo_tr[:, :neurons]
    next_c = halo_tr[:, 2 * neurons :]
    outside = jnp.dot(prev_c, gram_prev.T, precision=lax.Precision.HIGHEST) + jnp.dot(
        next_c, gram_next.T, precision=lax.Precision.HIGHEST
    )

    def sweep(group_id, current):
        offset = group_id * GROUP
        columns = lax.dynamic_slice_in_dim(gram_own, offset, GROUP, 1)
        coupled = jnp.dot(
            current, columns, precision=lax.Precision.HIGHEST
        ) + lax.dynamic_slice_in_dim(outside, offset, GROUP, 1)
        before = lax.dynamic_slice_in_dim(current, offset, GROUP, 1)
        driven = lax.dynamic_slice_in_dim(drive, offset, GROUP, 1)
        scaled = lax.dynamic_slice_in_dim(diag_own, offset, GROUP, 0)
        updated = jnp.maximum(before + (driven - coupled) / scaled, 0.0)
        return lax.dynamic_update_slice_in_dim(current, updated, offset, 1)

    new_tr = lax.fori_loop(0, GROUPS_DEV, sweep, start_tr)
    rounded = new_tr.astype(jnp.bfloat16)
    side_tr = with_halo(rounded, (("slab", 1),), neurons)
    frames_all = lax.all_gather(side_tr, "tm", axis=0, tiled=True)
    prev_all = frames_all[:, :neurons]
    own_all = frames_all[:, neurons : 2 * neurons]
    next_all = frames_all[:, 2 * neurons :]
    q_own = contract_first(own_all, own_all)
    q_prev = contract_first(prev_all, own_all)
    q_next = contract_first(next_all, own_all)
    divisor = jnp.maximum(jnp.diagonal(q_own), 1.0)
    share_rows = extended // lax.axis_size("tm")
    first_row = lax.axis_index("tm") * share_rows
    blocks = lax.all_to_all(movie_ext, "tm", split_axis=1, concat_axis=0, tiled=True)
    proj_rows = contract_first(blocks, own_all)
    zero_rows = jnp.zeros((voxels, neurons), jnp.bfloat16)
    prev_full = jnp.concatenate([prev_rim, zero_rows], 0)
    next_full = jnp.concatenate([zero_rows, next_edge], 0)
    foot_share = lax.dynamic_slice_in_dim(masked_foot, first_row, share_rows, 0).astype(jnp.float32)
    prev_share = lax.dynamic_slice_in_dim(prev_full, first_row, share_rows, 0).astype(jnp.float32)
    next_share = lax.dynamic_slice_in_dim(next_full, first_row, share_rows, 0).astype(jnp.float32)
    coupling = jnp.dot(foot_share, q_own, precision=lax.Precision.HIGHEST)
    coupling = coupling + jnp.dot(prev_share, q_prev, precision=lax.Precision.HIGHEST)
    coupling = coupling + jnp.dot(next_share, q_next, precision=lax.Precision.HIGHEST)
    new_foot = jnp.maximum(foot_share + (proj_rows - coupling) / divisor, 0.0).astype(jnp.bfloat16)
    return (new_tr, new_foot)


def solution(mesh):
    placed = (P("tm", "slab"), P(None, "slab"), P("tm", "slab"), P())
    return jax.shard_map(
        on_device,
        mesh=mesh,
        in_specs=placed,
        out_specs=(P("tm", "slab"), P("tm", "slab")),
        check_vma=False,
    )
```

profile of v0, /device:TPU:32, one launch (start us, length us, event | category | flops | bytes accessed | tf_op | source)
XLA Modules:
  0.0 112.4 jit_solution(6685149426623411708)
XLA Ops:
  0.6 1.3 %fusion.26 = s32[]{:T(128)} fusion(s32[32]{0:T(128)} %param.9, s32[]{:T(128)S(6)} %axis_index.23), kind=kLoop, calls=%fused_computation.45 | loop fusion | flops 95 | bytes 136 | tf_op jit(solution)/shard_map/reduce_sum | solution.py:47
  1.9 0.6 iota_compare_fusion.1
  2.6 0.8 broadcast_select_fusion
  3.4 3.9 %collective-permute-start.3 = (f32[64,256]{1,0:T(8,128)S(1)}, f32[64,256]{1,0:T(8,128)S(1)}, u32[]{:S(2)}, u32[]{:S(2)}) collective-permute-start(f32[64,256]{1,0:T(8,128)S(1)} %broadcast_select_fusion), channel_id=1, source_target_pairs={{8,0},{16,8},{24,16},{32,24},{40,32},{48,40},{56,48},{64,56},{72,6... | collective-permute-start | bytes 196616 | tf_op jit(solution)/shard_map/ppermute | solution.py:26
  7.3 1.9 %collective-permute-start.1 = (f32[64,256]{1,0:T(8,128)S(1)}, f32[64,256]{1,0:T(8,128)S(1)}, u32[]{:S(2)}, u32[]{:S(2)}) collective-permute-start(f32[64,256]{1,0:T(8,128)S(1)} %broadcast_select_fusion), channel_id=1, source_target_pairs={{0,8},{8,16},{16,24},{24,32},{32,40},{40,48},{48,56},{56,64},{64,7... | collective-permute-start | bytes 196616 | tf_op jit(solution)/shard_map/ppermute | solution.py:24
  9.3 0.0 copy-start.1
  9.3 2.3 %and_select_fusion = bf16[2176,256]{1,0:T(8,128)(2,1)S(1)} fusion(bf16[2176,256]{1,0:T(8,128)(2,1)} %param.7, pred[256]{0:T(512)(128)(4,1)S(1)} %iota_compare_fusion.1, pred[2176]{0:T(1024)(128)(4,1)S(1)} %fusion.22), kind=kLoop, calls=%fused_computation.11 | loop fusion | flops 1114112 | bytes 2230656 | tf_op jit(solution)/shard_map/jit(_where)/select_n | solution.py:51
  11.6 5.8 %collective-permute-start.4 = (bf16[128,256]{1,0:T(8,128)(2,1)S(1)}, bf16[128,256]{1,0:T(8,128)(2,1)S(1)}, u32[]{:S(2)}, u32[]{:S(2)}) collective-permute-start(bf16[128,256]{1,0:T(8,128)(2,1)S(1)} %get-tuple-element.125), channel_id=1, source_target_pairs={{8,0},{16,8},{24,16},{32,24},{40,32},{48,40},{56,48},{64,56},{72,6... | collective-permute-start | bytes 196616 | tf_op jit(solution)/shard_map/ppermute | solution.py:13
  17.3 1.9 %collective-permute-start.2 = (bf16[128,256]{1,0:T(8,128)(2,1)S(1)}, bf16[128,256]{1,0:T(8,128)(2,1)S(1)}, u32[]{:S(2)}, u32[]{:S(2)}) collective-permute-start(bf16[128,256]{1,0:T(8,128)(2,1)S(1)} %get-tuple-element.124), channel_id=1, source_target_pairs={{0,8},{8,16},{16,24},{24,32},{32,40},{40,48},{48,56},{56,64},{64,7... | collective-permute-start | bytes 196616 | tf_op jit(solution)/shard_map/ppermute | solution.py:13
  19.3 0.0 copy-done.1
  19.3 5.8 %collective-permute-start = (bf16[64,128]{1,0:T(8,128)(2,1)S(1)}, bf16[64,128]{1,0:T(8,128)(2,1)S(1)}, u32[]{:S(2)}, u32[]{:S(2)}) collective-permute-start(bf16[64,128]{1,0:T(8,128)(2,1)S(1)} %slice.20), channel_id=1, source_target_pairs={{8,0},{16,8},{24,16},{32,24},{40,32},{48,40},{56,48},{64,56},{72,6... | collective-permute-start | bytes 49160 | tf_op jit(solution)/shard_map/ppermute | solution.py:13
  25.1 0.5 fusion.35
  25.6 2.3 %gather_fusion = f32[256]{0:T(256)S(1)} fusion(f32[256,256]{1,0:T(8,128)S(1)} %fusion.35, s32[256]{0:T(256)S(1)} %bitcast.35), kind=kCustom, calls=%fused_computation | custom fusion | bytes 4096 | tf_op jit(solution)/shard_map/jit(diagonal)/cond/branch_0_fun/gather | solution.py:62
  28.0 0.0 collective-permute-done
  28.0 0.3 fusion.34
  28.3 0.0 collective-permute-done.4
  28.3 0.2 fusion.29
  28.5 0.0 collective-permute-done.2
  28.5 0.2 fusion.31
  28.8 0.0 collective-permute-done.3
  28.8 0.4 fusion.36
  29.1 0.0 collective-permute-done.1
  29.1 0.4 convolution_add_fusion.2
  29.5 0.7 while.13
  29.5 0.1 dynamic_slice.68
  29.6 0.2 fusion.57
  29.9 0.1 dynamic_slice.68
  29.9 0.2 fusion.57
  30.2 0.0 copy-start
  30.2 1.9 %collective-permute-start.5 = (bf16[64,256]{1,0:T(8,128)(2,1)S(1)}, bf16[64,256]{1,0:T(8,128)(2,1)S(1)}, u32[]{:S(2)}, u32[]{:S(2)}) collective-permute-start(bf16[64,256]{1,0:T(8,128)(2,1)S(1)} %convert_element_type.12), channel_id=1, source_target_pairs={{0,8},{8,16},{16,24},{24,32},{32,40},{40,48},{48,56},{56,64},{64,7... | collective-permute-start | bytes 98312 | tf_op jit(solution)/shard_map/ppermute | solution.py:24
  32.2 5.8 %collective-permute-start.6 = (bf16[64,256]{1,0:T(8,128)(2,1)S(1)}, bf16[64,256]{1,0:T(8,128)(2,1)S(1)}, u32[]{:S(2)}, u32[]{:S(2)}) collective-permute-start(bf16[64,256]{1,0:T(8,128)(2,1)S(1)} %convert_element_type.12), channel_id=1, source_target_pairs={{8,0},{16,8},{24,16},{32,24},{40,32},{48,40},{56,48},{64,56},{72,6... | collective-permute-start | bytes 98312 | tf_op jit(solution)/shard_map/ppermute | solution.py:26
  37.9 0.5 all_to_all.14
  38.4 0.8 copy.6
  39.2 0.0 copy-done
  39.2 10.9 %all-to-all-start = ((bf16[64,8,272]{2,0,1:T(8,128)(2,1)}), bf16[64,8,272]{2,0,1:T(8,128)(2,1)S(1)}, u32[]{:S(2)}, u32[]{:S(2)}) async-start(bf16[64,8,272]{2,0,1:T(8,128)(2,1)} %copy.6), calls=%async_computation | async-start | bytes 786432 | tf_op jit(solution)/shard_map/all_to_all | solution.py:95
  50.1 0.0 collective-permute-done.5
  50.1 0.0 collective-permute-done.6
  50.2 57.1 %all_gather.3 = bf16[512,768]{1,0:T(8,128)(2,1)S(1)} all-gather(bf16[64,768]{1,0:T(8,128)(2,1)S(1)} %pad_maximum_fusion), channel_id=1, replica_groups=mesh['slab'=32,'tm'=8] {'tm'}, dimensions={0}, use_global_device_ids=true | all-gather | bytes 884736 | tf_op jit(solution)/shard_map/all_gather | solution.py:85
  107.3 0.3 fusion.17
  107.5 0.3 fusion.13
  107.8 2.3 %gather_fusion.1 = f32[256]{0:T(256)S(1)} fusion(f32[256,256]{1,0:T(8,128)S(1)} %fusion.17, s32[256]{0:T(256)S(1)} %bitcast.36), kind=kCustom, calls=%fused_computation.1 | custom fusion | bytes 4096 | tf_op jit(solution)/shard_map/jit(diagonal)/cond/branch_0_fun/gather | solution.py:92
  110.1 0.3 fusion.20
  110.5 0.3 convolution_add_fusion.1
  110.8 0.3 fusion.11
  111.1 0.4 convolution_add_fusion
  111.4 0.0 all-to-all-done
  111.4 0.9 fusion.10
  (12 shorter events, 0.1 us)
Async XLA Ops:
  3.4 25.3 %collective-permute-start.3 = (f32[64,256]{1,0:T(8,128)S(1)}, f32[64,256]{1,0:T(8,128)S(1)}, u32[]{:S(2)}, u32[]{:S(2)}) collective-permute-start(f32[64,256]{1,0:T(8,128)S(1)} %broadcast_select_fusion), channel_id=1, source_target_pairs={{8,0},{16,8},{24,16},{32,24},{40,32},{48,40},{56,48},{64,56},{72,6... | collective-permute-start | bytes 196616 | tf_op jit(solution)/shard_map/ppermute | solution.py:26
  7.3 21.8 %collective-permute-start.1 = (f32[64,256]{1,0:T(8,128)S(1)}, f32[64,256]{1,0:T(8,128)S(1)}, u32[]{:S(2)}, u32[]{:S(2)}) collective-permute-start(f32[64,256]{1,0:T(8,128)S(1)} %broadcast_select_fusion), channel_id=1, source_target_pairs={{0,8},{8,16},{16,24},{24,32},{32,40},{40,48},{48,56},{56,64},{64,7... | collective-permute-start | bytes 196616 | tf_op jit(solution)/shard_map/ppermute | solution.py:24
  9.3 10.0 %copy-start.1 = (bf16[64,2048]{1,0:T(8,128)(2,1)S(1)}, bf16[64,2048]{1,0:T(8,128)(2,1)}, u32[]{:S(2)}) copy-start(bf16[64,2048]{1,0:T(8,128)(2,1)} %param.6) | copy-start | bytes 786436
  11.6 16.7 %collective-permute-start.4 = (bf16[128,256]{1,0:T(8,128)(2,1)S(1)}, bf16[128,256]{1,0:T(8,128)(2,1)S(1)}, u32[]{:S(2)}, u32[]{:S(2)}) collective-permute-start(bf16[128,256]{1,0:T(8,128)(2,1)S(1)} %get-tuple-element.125), channel_id=1, source_target_pairs={{8,0},{16,8},{24,16},{32,24},{40,32},{48,40},{56,48},{64,56},{72,6... | collective-permute-start | bytes 196616 | tf_op jit(solution)/shard_map/ppermute | solution.py:13
  17.3 11.2 %collective-permute-start.2 = (bf16[128,256]{1,0:T(8,128)(2,1)S(1)}, bf16[128,256]{1,0:T(8,128)(2,1)S(1)}, u32[]{:S(2)}, u32[]{:S(2)}) collective-permute-start(bf16[128,256]{1,0:T(8,128)(2,1)S(1)} %get-tuple-element.124), channel_id=1, source_target_pairs={{0,8},{8,16},{16,24},{24,32},{32,40},{40,48},{48,56},{56,64},{64,7... | collective-permute-start | bytes 196616 | tf_op jit(solution)/shard_map/ppermute | solution.py:13
  19.3 8.7 %collective-permute-start = (bf16[64,128]{1,0:T(8,128)(2,1)S(1)}, bf16[64,128]{1,0:T(8,128)(2,1)S(1)}, u32[]{:S(2)}, u32[]{:S(2)}) collective-permute-start(bf16[64,128]{1,0:T(8,128)(2,1)S(1)} %slice.20), channel_id=1, source_target_pairs={{8,0},{16,8},{24,16},{32,24},{40,32},{48,40},{56,48},{64,56},{72,6... | collective-permute-start | bytes 49160 | tf_op jit(solution)/shard_map/ppermute | solution.py:13
  30.2 9.0 %copy-start = (f32[64,256]{1,0:T(8,128)}, f32[64,256]{1,0:T(8,128)S(1)}, u32[]{:S(2)}) copy-start(f32[64,256]{1,0:T(8,128)S(1)} %get-tuple-element.109) | copy-start | bytes 196612
  30.2 19.9 %collective-permute-start.5 = (bf16[64,256]{1,0:T(8,128)(2,1)S(1)}, bf16[64,256]{1,0:T(8,128)(2,1)S(1)}, u32[]{:S(2)}, u32[]{:S(2)}) collective-permute-start(bf16[64,256]{1,0:T(8,128)(2,1)S(1)} %convert_element_type.12), channel_id=1, source_target_pairs={{0,8},{8,16},{16,24},{24,32},{32,40},{40,48},{48,56},{56,64},{64,7... | collective-permute-start | bytes 98312 | tf_op jit(solution)/shard_map/ppermute | solution.py:24
  32.2 18.0 %collective-permute-start.6 = (bf16[64,256]{1,0:T(8,128)(2,1)S(1)}, bf16[64,256]{1,0:T(8,128)(2,1)S(1)}, u32[]{:S(2)}, u32[]{:S(2)}) collective-permute-start(bf16[64,256]{1,0:T(8,128)(2,1)S(1)} %convert_element_type.12), channel_id=1, source_target_pairs={{8,0},{16,8},{24,16},{32,24},{40,32},{48,40},{56,48},{64,56},{72,6... | collective-permute-start | bytes 98312 | tf_op jit(solution)/shard_map/ppermute | solution.py:26
  39.2 72.2 %all-to-all-start = ((bf16[64,8,272]{2,0,1:T(8,128)(2,1)}), bf16[64,8,272]{2,0,1:T(8,128)(2,1)S(1)}, u32[]{:S(2)}, u32[]{:S(2)}) async-start(bf16[64,8,272]{2,0,1:T(8,128)(2,1)} %copy.6), calls=%async_computation | async-start | bytes 786432 | tf_op jit(solution)/shard_map/all_to_all | solution.py:95
where the time goes:
time: 113 us; the launch traced here: 112 us
  blocking collectives  57.1 us (51%)
  starting transfers between devices  37.8 us (33%)
  local copies, waits for them, and re-layouts  6.19 us (5%)
  matrix products  5.12 us (5%)
  other arithmetic  5.09 us (5%)
    all_gather x1, blocking collectives, on_device(): frames_all = lax.all_gather(side_tr, 'tm', axis=0, tiled=True)  57.1 us
    ppermute x3, starting transfers between devices, passed_along(): return lax.ppermute(block, axis, route)  13.4 us
    all_to_all x1, starting transfers between devices, on_device(): lax.all_to_all(movie_ext, 'tm', split_axis=1, concat_axis=0, tiled=True)  10.9 us
    ppermute x2, starting transfers between devices, with_halo(): lax.ppermute(head, axis, [((i + 1) % count, i) for i in range(ends)])  9.65 us
    ppermute x2, starting transfers between devices, with_halo(): lax.ppermute(tail, axis, [(i, (i + 1) % count) for i in range(ends)])  3.84 us
    dot_general x7, matrix products, contract_first(): lax.dot_general(left, right, (((0,), (0,)), ((), ())), preferred_element_...  2.64 us
    gather x1, local copies, waits for them, and re-layouts, on_device(): divisor = jnp.maximum(jnp.diagonal(q_own), 1.0)  2.34 us
    gather x1, local copies, waits for them, and re-layouts, on_device(): diag_own = jnp.diagonal(gram_own) + 1e-06  2.34 us
  transfers between devices with their start and end apart: 8, of which 0 were waited for; matrix products, arithmetic and copies ran while one was open for 10% of the time, Pallas kernels for 0%

commit v1 on v0

v1 whole, which is shorter than its diff:
```python
import functools

import jax
import jax.numpy as jnp
from jax import lax
from jax.experimental import pallas as pl
from jax.experimental.pallas import tpu as pltpu
from jax.sharding import PartitionSpec as P

MESH = pl.DeviceIdType.MESH
F32 = jnp.float32
BF16 = jnp.bfloat16
GROUP = 128


def dot(a, b, ca=1, cb=0, precision=None):
    return lax.dot_general(
        a, b, (((ca,), (cb,)), ((), ())), preferred_element_type=F32, precision=precision
    )


def halves(x):
    high = x.astype(BF16)
    return high, (x - high.astype(F32)).astype(BF16)


def remote(src, dst, sems, index, **device):
    return pltpu.make_async_remote_copy(
        src_ref=src,
        dst_ref=dst,
        send_sem=sems[0].at[index[0]],
        recv_sem=sems[1].at[index[1]],
        device_id=device,
        device_id_type=MESH,
    )


def exchange_kernel(
    dims,
    live_ref, y_hbm, a_hbm, c_hbm,
    tr_out, b_all, yt_out, side_out, share_out,
    yv, av, cv, y_send, y_recv, rim_in, head_out, tail_out, head_in, tail_in,
    side_head, side_tail,
    load_sem, y_ss, y_rs, b_ss, b_rs, h_ss, h_rs, s_ss, s_rs,
):
    slabs, parts, frames, voxels, rows, neurons = dims
    rim = rows - voxels
    share = rows // parts
    wide = share // 128 * 128
    rest = share - wide
    s = lax.axis_index("slab")
    t = lax.axis_index("tm")
    has_next = s < slabs - 1
    has_prev = s > 0
    first, last = t == 0, t == parts - 1

    loads = [
        pltpu.make_async_copy(c_hbm, cv, load_sem.at[0]),
        pltpu.make_async_copy(a_hbm.at[:rim], av.at[:rim], load_sem.at[1]),
        pltpu.make_async_copy(a_hbm.at[voxels:], av.at[voxels:], load_sem.at[2]),
        pltpu.make_async_copy(y_hbm, yv, load_sem.at[3]),
        pltpu.make_async_copy(a_hbm.at[rim:voxels], av.at[rim:voxels], load_sem.at[4]),
    ]
    for load in loads:
        load.start()

    barrier = pltpu.get_barrier_semaphore()

    def greet(**device):
        pl.semaphore_signal(barrier, inc=1, device_id=device, device_id_type=MESH)

    for i in range(1, parts):
        greet(tm=lax.rem(t + i, parts))

    @pl.when(has_next)
    def _():
        greet(slab=s + 1)

    @pl.when(has_prev)
    def _():
        greet(slab=s - 1)

    @pl.when(first & has_prev)
    def _():
        for i in range(1, parts):
            greet(slab=s - 1, tm=t + i)

    @pl.when(last & has_next)
    def _():
        for i in range(1, parts):
            greet(slab=s + 1, tm=t - i)

    one = jnp.int32(1)
    zero = jnp.int32(0)
    pl.semaphore_wait(
        barrier,
        parts - 1
        + jnp.where(has_next, jnp.where(first, one, one + 1), zero)
        + jnp.where(has_prev, jnp.where(last, one, one + 1), zero),
    )

    rim_copy = remote(y_hbm.at[:, :rim], rim_in, (h_ss, h_rs), (0, 0), slab=s - 1)
    head_copy = remote(head_out, head_in, (h_ss, h_rs), (1, 1), slab=s - 1)
    tail_copy = remote(tail_out, tail_in, (h_ss, h_rs), (2, 2), slab=s + 1)

    @pl.when(has_prev)
    def _():
        rim_copy.start()

    live = lax.broadcasted_iota(jnp.int32, (1, neurons), 1) < live_ref[s]
    for load in loads[:3]:
        load.wait()
    keep_tail = jnp.where(has_next, 1.0, 0.0).astype(F32)
    start = jnp.where(live, cv[...], 0.0)
    c_high, c_low = halves(start)
    head = av[:rim]
    tail = (av[voxels:].astype(F32) * keep_tail).astype(BF16)
    av[voxels:] = tail
    head_out[...] = dot(c_high, head, 1, 1) + dot(c_low, head, 1, 1)
    tail_out[...] = dot(c_high, tail, 1, 1) + dot(c_low, tail, 1, 1)

    @pl.when(has_prev)
    def _():
        head_copy.start()

    @pl.when(has_next)
    def _():
        tail_copy.start()

    loads[3].wait()
    y_copies = []

    def pack(p, span, last_tile):
        base = p * share - p * share // 128 * 128
        for k in range(wide // 128):
            y_send[p, k * frames : (k + 1) * frames] = span[:, base + k * 128 : base + (k + 1) * 128]

    group = lax.broadcasted_iota(jnp.int32, (1, 128), 1) // rest
    left = jnp.zeros((frames, 128), F32)
    for p in range(parts - 1):
        tile0 = p * share // 128
        pack(p, yv[:, tile0 * 128 : (tile0 + 3) * 128], None)
        left = jnp.where(group == p, yv[:, (tile0 + 2) * 128 : (tile0 + 3) * 128].astype(F32), left)
    left_t = left.T.astype(BF16)
    for p in range(parts - 1):
        y_send[p, wide // 128 * frames :, :frames] = left_t[p * rest : (p + 1) * rest]

    for i in range(1, parts):
        to = lax.rem(t + i, parts)
        copy = remote(y_send.at[to], y_recv.at[i], (y_ss, y_rs), (i, i), tm=to)
        y_copies.append((to, copy))

        @pl.when(to < parts - 1)
        def _(copy=copy):
            copy.start()

    @pl.when(has_next)
    def _():
        rim_copy.wait_recv()

    @pl.when(jnp.logical_not(has_next))
    def _():
        rim_in[...] = jnp.zeros_like(rim_in)

    rim_y = rim_in[...]
    p = parts - 1
    tile0 = p * share // 128
    span = jnp.concatenate([yv[:, tile0 * 128 :], rim_y], 1)
    pack(p, span, None)
    y_send[p, wide // 128 * frames :, :frames] = rim_y.astype(F32).T.astype(BF16)[p * rest :]
    for to, copy in y_copies:

        @pl.when(to == parts - 1)
        def _(copy=copy):
            copy.start()

    loads[4].wait()
    foot = av[...]
    gram = dot(foot, foot, 0, 0)
    eye = lax.broadcasted_iota(jnp.int32, (neurons, neurons), 0) == lax.broadcasted_iota(
        jnp.int32, (neurons, neurons), 1
    )
    scale = jnp.sum(jnp.where(eye, gram, 0.0), 0, keepdims=True) + 1e-6
    own_drive = dot(jnp.concatenate([yv[...], rim_y], 1), foot)
    coupled = dot(start, gram, precision=lax.Precision.HIGHEST)
    base = own_drive - coupled

    @pl.when(has_next)
    def _():
        head_copy.wait_recv()

    @pl.when(has_prev)
    def _():
        tail_copy.wait_recv()

    @pl.when(jnp.logical_not(has_next))
    def _():
        head_in[...] = jnp.zeros_like(head_in)

    @pl.when(jnp.logical_not(has_prev))
    def _():
        tail_in[...] = jnp.zeros_like(tail_in)

    nh, nl = halves(head_in[...])
    ph, pw = halves(tail_in[...])
    outside = dot(
        jnp.concatenate([nh, nl, ph, pw], 1), jnp.concatenate([tail, tail, head, head], 0)
    )
    base = base - outside
    done = []
    for g in range(neurons // GROUP):
        cut = slice(g * GROUP, (g + 1) * GROUP)
        change = base[:, cut]
        for h in range(g):
            moved = done[h] - start[:, h * GROUP : (h + 1) * GROUP]
            change = change - dot(
                moved, gram[h * GROUP : (h + 1) * GROUP, cut], precision=lax.Precision.HIGHEST
            )
        done.append(
            jnp.where(
                live[:, cut], jnp.maximum(start[:, cut] + change / scale[:, cut], 0.0), 0.0
            )
        )
    new_tr = jnp.concatenate(done, 1)
    rounded = new_tr.astype(BF16)
    b_all[0] = rounded

    b_copies = []
    for i in range(1, parts):
        to = lax.rem(t + i, parts)
        copy = remote(b_all.at[0], b_all.at[i], (b_ss, b_rs), (i, i), tm=to)
        copy.start()
        b_copies.append(copy)

    side_head[...] = dot(rounded, head, 1, 1).astype(BF16)
    side_tail[...] = dot(rounded, tail, 1, 1).astype(BF16)
    to_first = lax.rem(parts - t, parts)
    to_last = parts - 1 - t
    tail_side = remote(
        side_tail, side_out.at[to_first], (s_ss, s_rs), (0, to_first), slab=s + 1, tm=t * 0
    )
    head_side = remote(
        side_head, side_out.at[to_last], (s_ss, s_rs), (1, to_last), slab=s - 1, tm=t * 0 + parts - 1
    )

    @pl.when(has_next)
    def _():
        tail_side.start()

    @pl.when(has_prev)
    def _():
        head_side.start()

    tr_out[...] = new_tr
    row0 = pl.multiple_of(t * share, 16)
    row = row0 + lax.broadcasted_iota(jnp.int32, (share, 1), 0)
    mine = av[pl.ds(row0, share)].astype(F32)
    share_out[...] = jnp.where(live & (row < rows), mine, 0.0).astype(BF16)

    y_recv[0] = y_send[t]
    for to, copy in y_copies:
        copy.wait_recv()
    per = wide // 128
    for k in range(per):
        block = y_recv[:, k * frames : (k + 1) * frames].reshape(parts * frames, 128)
        yt_out[k * 128 : (k + 1) * 128] = block.T
    yt_out[wide:] = jnp.concatenate(
        [y_recv[i, per * frames :, :frames] for i in range(parts)], 1
    )

    @pl.when((first & has_prev) | (last & has_next))
    def _():
        for i in range(parts):
            remote(side_tail, side_out.at[i], (s_ss, s_rs), (0, i), slab=s).wait_recv()

    @pl.when(jnp.logical_not((first & has_prev) | (last & has_next)))
    def _():
        side_out[...] = jnp.zeros_like(side_out)

    for copy in b_copies:
        copy.wait_recv()
    for to, copy in y_copies:
        copy.wait_send()
    for copy in b_copies:
        copy.wait_send()

    @pl.when(has_prev)
    def _():
        rim_copy.wait_send()
        head_copy.wait_send()
        head_side.wait_send()

    @pl.when(has_next)
    def _():
        tail_copy.wait_send()
        tail_side.wait_send()


def update_kernel(dims, live_ref, tr, b_all, yt, side, mine, tr_hbm, foot_out, delta, sem):
    slabs, parts, frames, voxels, rows, neurons = dims
    rim = rows - voxels
    share = rows // parts
    s = lax.axis_index("slab")
    t = lax.axis_index("tm")
    store = pltpu.make_async_copy(tr, tr_hbm, sem)
    store.start()
    live = lax.broadcasted_iota(jnp.int32, (1, neurons), 1) < live_ref[s]
    own = b_all[...].reshape(parts * frames, neurons)
    q = dot(own, own, 0, 0)
    delta[...] = dot(yt[...], own)

    @pl.when(t == 0)
    def _():
        delta[:rim] = delta[:rim] - dot(side[...].reshape(parts * frames, rim), own, 0, 0)

    @pl.when(t == parts - 1)
    def _():
        delta[share - rim :] = delta[share - rim :] - dot(
            side[...].reshape(parts * frames, rim), own, 0, 0
        )

    eye = lax.broadcasted_iota(jnp.int32, (neurons, neurons), 0) == lax.broadcasted_iota(
        jnp.int32, (neurons, neurons), 1
    )
    scale = jnp.maximum(jnp.sum(jnp.where(eye, q, 0.0), 0, keepdims=True), 1.0)
    q_high, q_low = halves(q)
    base = mine[...]
    coupling = dot(base, q_high) + dot(base, q_low)
    foot_out[...] = jnp.maximum(base.astype(F32) + (delta[...] - coupling) / scale, 0.0).astype(
        BF16
    )
    store.wait()


def solution(mesh):
    slabs, parts = mesh.shape["slab"], mesh.shape["tm"]

    def on_device(recording, footprints, traces, live_count):
        frames, voxels = recording.shape
        rows, neurons = footprints.shape
        rim = rows - voxels
        share = rows // parts
        dims = (slabs, parts, frames, voxels, rows, neurons)
        hbm = pl.BlockSpec(memory_space=pltpu.HBM)
        vmem = pl.BlockSpec(memory_space=pltpu.VMEM)
        smem = pl.BlockSpec(memory_space=pltpu.SMEM)
        packed = share // 128 * frames + share % 128
        dma = pltpu.SemaphoreType.DMA
        tr, b_all, yt, side, mine = pl.pallas_call(
            functools.partial(exchange_kernel, dims),
            out_shape=[
                pltpu.VMEM((frames, neurons), F32),
                pltpu.VMEM((parts, frames, neurons), BF16),
                pltpu.VMEM((share, parts * frames), BF16),
                pltpu.VMEM((parts, frames, rim), BF16),
                pltpu.VMEM((share, neurons), BF16),
            ],
            in_specs=[smem, hbm, hbm, hbm],
            out_specs=[vmem] * 5,
            scratch_shapes=[
                pltpu.VMEM((frames, voxels), BF16),
                pltpu.VMEM((rows, neurons), BF16),
                pltpu.VMEM((frames, neurons), F32),
                pltpu.VMEM((parts, packed, 128), BF16),
                pltpu.VMEM((parts, packed, 128), BF16),
                pltpu.VMEM((frames, rim), BF16),
                pltpu.VMEM((frames, rim), F32),
                pltpu.VMEM((frames, rim), F32),
                pltpu.VMEM((frames, rim), F32),
                pltpu.VMEM((frames, rim), F32),
                pltpu.VMEM((frames, rim), BF16),
                pltpu.VMEM((frames, rim), BF16),
                dma((5,)),
                dma((parts,)),
                dma((parts,)),
                dma((parts,)),
                dma((parts,)),
                dma((3,)),
                dma((3,)),
                dma((2,)),
                dma((parts,)),
            ],
            compiler_params=pltpu.CompilerParams(
                collective_id=0, has_side_effects=True, vmem_limit_bytes=32 * 2**20
            ),
            name="exchange",
        )(live_count, recording, footprints, traces)
        return pl.pallas_call(
            functools.partial(update_kernel, dims),
            out_shape=[
                jax.ShapeDtypeStruct((frames, neurons), F32),
                jax.ShapeDtypeStruct((share, neurons), BF16),
            ],
            in_specs=[smem] + [vmem] * 5,
            out_specs=[hbm, vmem],
            scratch_shapes=[pltpu.VMEM((share, neurons), F32), dma],
            compiler_params=pltpu.CompilerParams(vmem_limit_bytes=32 * 2**20),
            name="update",
        )(live_count, tr, b_all, yt, side, mine)

    placed = (P("tm", "slab"), P(None, "slab"), P("tm", "slab"), P())
    return jax.shard_map(
        on_device,
        mesh=mesh,
        in_specs=placed,
        out_specs=(P("tm", "slab"), P("tm", "slab")),
        check_vma=False,
    )
```

time: 113 us -> 34.9 us (0.31)
  blocking collectives: 57.1 us -> 0 us
  starting transfers between devices: 37.8 us -> 0 us
  Pallas kernels: 0 us -> 30.4 us
  matrix products: 5.12 us -> 0 us
  other arithmetic: 5.09 us -> 0 us
  local copies, waits for them, and re-layouts: 6.19 us -> 3.68 us
    all_gather x1 -> x0, blocking collectives: 57.1 us -> none  [on_device(): frames_all = lax.all_gather(side_tr, 'tm', axis=0, tiled=True)]
    pallas_call x0 -> x2, Pallas kernels: none -> 30.4 us  [the longest x1 28.4 us: on_device(): pl.pallas_call(functools.partial(exchange_kernel, dims), out_shape=[pltpu...]
    ppermute x7 -> x0, starting transfers between devices: 26.9 us -> none  [the longest x3 13.4 us: passed_along(): return lax.ppermute(block, axis, route)]
    all_to_all x1 -> x0, starting transfers between devices: 10.9 us -> none  [on_device(): lax.all_to_all(movie_ext, 'tm', split_axis=1, concat_axis=0, tiled=True)]
    dot_general x15 -> x0, matrix products: 5.12 us -> none  [the longest x7 2.64 us: contract_first(): lax.dot_general(left, right, (((0,), (0,)), ((), ())), preferred_element_...]
    gather x2 -> x0, local copies, waits for them, and re-layouts: 4.69 us -> none  [the longest x1 2.34 us: on_device(): divisor = jnp.maximum(jnp.diagonal(q_own), 1.0)]
    unnamed x5 -> x8, local copies, waits for them, and re-layouts: 0.03 us -> 3.68 us
    select_n x2 -> x0, other arithmetic: 3.11 us -> none  [the longest x1 2.26 us: on_device(): masked_foot = jnp.where(kept_mask, footprints, jnp.zeros_like(footprints))]
  transfers between devices with their start and end apart: 8 -> 0, of which waited for: 0 -> 0; matrix products, arithmetic and copies ran while one was open for 10% -> 0% of each run, Pallas kernels for 0% -> 0%
where the time goes in v1:
time: 34.9 us; the launch traced here: 34.7 us
  Pallas kernels  30.4 us (87%)
  local copies, waits for them, and re-layouts  3.68 us (11%)
  between operations  0.65 us (2%)
    pallas_call x1, Pallas kernels, on_device(): pl.pallas_call(functools.partial(exchange_kernel, dims), out_shape=[pltpu...  28.4 us
    unnamed x8, local copies, waits for them, and re-layouts  3.68 us
    pallas_call x1, Pallas kernels, on_device(): pl.pallas_call(functools.partial(update_kernel, dims), out_shape=[jax.Sha...  2 us

profile of v1, /device:TPU:32, one launch (start us, length us, event | category | flops | bytes accessed | tf_op | source)
XLA Modules:
  0.0 34.7 jit_solution(18258000728941545268)
XLA Ops:
  0.6 0.0 copy-start
  0.6 1.2 %copy-done = bf16[2176,256]{1,0:T(8,128)(2,1)S(1)} copy-done((bf16[2176,256]{1,0:T(8,128)(2,1)S(1)}, bf16[2176,256]{1,0:T(8,128)(2,1)}, u32[]{:S(2)}) %copy-start) | copy-done | bytes 1114136
  1.9 0.0 copy-start.1
  1.9 0.9 %copy-done.1 = bf16[64,2048]{1,0:T(8,128)(2,1)S(1)} copy-done((bf16[64,2048]{1,0:T(8,128)(2,1)S(1)}, bf16[64,2048]{1,0:T(8,128)(2,1)}, u32[]{:S(2)}) %copy-start.1) | copy-done | bytes 262168
  2.8 0.0 copy-start.2
  2.8 0.8 %copy-done.2 = f32[64,256]{1,0:T(8,128)S(1)} copy-done((f32[64,256]{1,0:T(8,128)S(1)}, f32[64,256]{1,0:T(8,128)}, u32[]{:S(2)}) %copy-start.2) | copy-done | bytes 65560
  3.7 0.0 copy-start.3
  3.7 0.7 %copy-done.3 = s32[32]{0:T(128)S(1)} copy-done((s32[32]{0:T(128)S(1)}, s32[32]{0:T(128)}, u32[]{:S(2)}) %copy-start.3) | copy-done | bytes 152
  4.3 28.4 %exchange.1 = (f32[64,256]{1,0:T(8,128)S(1)}, bf16[8,64,256]{2,1,0:T(8,128)(2,1)S(1)}, bf16[272,512]{1,0:T(8,128)(2,1)S(1)}, bf16[8,64,128]{2,1,0:T(8,128)(2,1)S(1)}, bf16[272,256]{1,0:T(8,128)(2,1)S(1)}) custom-call(s32[32]{0:T(128)S(1)} %copy-done.3, bf16[64,2048]{1,0:T(8,128)(2,1)S(1)} %copy-done.1, bf16[2176,256]{1,0:T(8,128)(2,1)S(1)} %copy-done, ...), custom_call_target="tpu_custom_call" | custom-call | tf_op jit(solution)/shard_map/exchange/pallas_call | solution.py:349
  32.7 2.0 %update.1 = (f32[64,256]{1,0:T(8,128)}, bf16[272,256]{1,0:T(8,128)(2,1)}) custom-call(s32[32]{0:T(128)S(1)} %copy-done.3, f32[64,256]{1,0:T(8,128)S(1)} %get-tuple-element.7.tr, bf16[8,64,256]{2,1,0:T(8,128)(2,1)S(1)} %get-tuple-element.8.b_all, bf16[272,512]{1,0:T(8,128)(2,1)S(1)} %get-tuple-element.9.yt, bf16[8,64,128]{2,1,0:T(8,128)(2,1)S(1)} %get-tuple-element.10.side, ...), custom_call_target="tpu_custom_call" | custom-call | tf_op jit(solution)/shard_map/update/pallas_call | solution.py:388
Async XLA Ops:
  0.6 1.2 %copy-start = (bf16[2176,256]{1,0:T(8,128)(2,1)S(1)}, bf16[2176,256]{1,0:T(8,128)(2,1)}, u32[]{:S(2)}) copy-start(bf16[2176,256]{1,0:T(8,128)(2,1)} %a_hbm.1) | copy-start | bytes 3342340
  1.9 0.9 %copy-start.1 = (bf16[64,2048]{1,0:T(8,128)(2,1)S(1)}, bf16[64,2048]{1,0:T(8,128)(2,1)}, u32[]{:S(2)}) copy-start(bf16[64,2048]{1,0:T(8,128)(2,1)} %y_hbm.1) | copy-start | bytes 786436
  2.8 0.8 %copy-start.2 = (f32[64,256]{1,0:T(8,128)S(1)}, f32[64,256]{1,0:T(8,128)}, u32[]{:S(2)}) copy-start(f32[64,256]{1,0:T(8,128)} %c_hbm.1) | copy-start | bytes 196612
  3.7 0.7 %copy-start.3 = (s32[32]{0:T(128)S(1)}, s32[32]{0:T(128)}, u32[]{:S(2)}) copy-start(s32[32]{0:T(128)} %live_ref.3) | copy-start | bytes 388

commit v2 on v1

--- a/solution.py
+++ b/solution.py
@@ -90,22 +90,9 @@
         for i in range(1, parts):
             greet(slab=s + 1, tm=t - i)
 
-    one = jnp.int32(1)
-    zero = jnp.int32(0)
-    pl.semaphore_wait(
-        barrier,
-        parts - 1
-        + jnp.where(has_next, jnp.where(first, one, one + 1), zero)
-        + jnp.where(has_prev, jnp.where(last, one, one + 1), zero),
-    )
-
     rim_copy = remote(y_hbm.at[:, :rim], rim_in, (h_ss, h_rs), (0, 0), slab=s - 1)
     head_copy = remote(head_out, head_in, (h_ss, h_rs), (1, 1), slab=s - 1)
     tail_copy = remote(tail_out, tail_in, (h_ss, h_rs), (2, 2), slab=s + 1)
-
-    @pl.when(has_prev)
-    def _():
-        rim_copy.start()
 
     live = lax.broadcasted_iota(jnp.int32, (1, neurons), 1) < live_ref[s]
     for load in loads[:3]:
@@ -119,6 +106,19 @@
     head_out[...] = dot(c_high, head, 1, 1) + dot(c_low, head, 1, 1)
     tail_out[...] = dot(c_high, tail, 1, 1) + dot(c_low, tail, 1, 1)
 
+    one = jnp.int32(1)
+    zero = jnp.int32(0)
+    pl.semaphore_wait(
+        barrier,
+        parts - 1
+        + jnp.where(has_next, jnp.where(first, one, one + 1), zero)
+        + jnp.where(has_prev, jnp.where(last, one, one + 1), zero),
+    )
+
+    @pl.when(has_prev)
+    def _():
+        rim_copy.start()
+
     @pl.when(has_prev)
     def _():
         head_copy.start()
@@ -145,8 +145,12 @@
     for p in range(parts - 1):
         y_send[p, wide // 128 * frames :, :frames] = left_t[p * rest : (p + 1) * rest]
 
-    for i in range(1, parts):
-        to = lax.rem(t + i, parts)
+    across = t + 1 - 2 * lax.rem(t, 2)
+    half = parts // 2
+    routes = [(1, across)]
+    routes += [(half + k, lax.rem(across + 2 * k, parts)) for k in range(1, half)]
+    routes += [(1 + k, lax.rem(t + 2 * k, parts)) for k in range(1, half)]
+    for i, to in routes:
         copy = remote(y_send.at[to], y_recv.at[i], (y_ss, y_rs), (i, i), tm=to)
         y_copies.append((to, copy))
 
@@ -225,17 +229,26 @@
     rounded = new_tr.astype(BF16)
     b_all[0] = rounded
 
+    along = [lax.rem(t + i, parts) for i in range(2, parts, 2)]
+    b_cross = remote(b_all.at[0], b_all.at[1], (b_ss, b_rs), (1, 1), tm=across)
+    b_cross.start()
     b_copies = []
-    for i in range(1, parts):
-        to = lax.rem(t + i, parts)
-        copy = remote(b_all.at[0], b_all.at[i], (b_ss, b_rs), (i, i), tm=to)
+    for n, to in enumerate(along):
+        copy = remote(b_all.at[0], b_all.at[2 + n], (b_ss, b_rs), (2 + n, 2 + n), tm=to)
         copy.start()
         b_copies.append(copy)
 
     side_head[...] = dot(rounded, head, 1, 1).astype(BF16)
     side_tail[...] = dot(rounded, tail, 1, 1).astype(BF16)
-    to_first = lax.rem(parts - t, parts)
-    to_last = parts - 1 - t
+    def slot_at(x_to, z_to):
+        away = lax.rem(x_to - t // 2 + parts, parts // 2)
+        same, here = lax.rem(t, 2) == z_to, away == 0
+        near = jnp.where(here, 0, 1 + away)
+        far = jnp.where(here, 1, parts // 2 + away)
+        return jnp.where(same, near, far)
+
+    to_first = slot_at(0, 0)
+    to_last = slot_at(parts // 2 - 1, 1)
     tail_side = remote(
         side_tail, side_out.at[to_first], (s_ss, s_rs), (0, to_first), slab=s + 1, tm=t * 0
     )
@@ -252,6 +265,11 @@
         head_side.start()
 
     tr_out[...] = new_tr
+    b_cross.wait_recv()
+    for n, to in enumerate(along):
+        copy = remote(b_all.at[1], b_all.at[5 + n], (b_ss, b_rs), (5 + n, 5 + n), tm=to)
+        copy.start()
+        b_copies.append(copy)
     row0 = pl.multiple_of(t * share, 16)
     row = row0 + lax.broadcasted_iota(jnp.int32, (share, 1), 0)
     mine = av[pl.ds(row0, share)].astype(F32)
@@ -281,6 +299,7 @@
         copy.wait_recv()
     for to, copy in y_copies:
         copy.wait_send()
+    b_cross.wait_send()
     for copy in b_copies:
         copy.wait_send()
 
@@ -381,7 +400,7 @@
                 dma((parts,)),
             ],
             compiler_params=pltpu.CompilerParams(
-                collective_id=0, has_side_effects=True, vmem_limit_bytes=32 * 2**20
+                collective_id=0, has_side_effects=True, vmem_limit_bytes=60 * 2**20
             ),
             name="exchange",
         )(live_count, recording, footprints, traces)

time: 34.9 us -> 27.4 us (0.79)
  Pallas kernels: 30.4 us -> 26.7 us
  local copies, waits for them, and re-layouts: 3.68 us -> 0.01 us
    pallas_call x1, Pallas kernels: 28.4 us -> 24.7 us  [on_device(): pl.pallas_call(functools.partial(exchange_kernel, dims), out_shape=[pltpu...]
    unnamed x8 -> x2, local copies, waits for them, and re-layouts: 3.68 us -> 0.01 us
where the time goes in v2:
time: 27.4 us; the launch traced here: 27.3 us
  Pallas kernels  26.7 us (97%)
  between operations  0.65 us (2%)
    pallas_call x1, Pallas kernels, on_device(): pl.pallas_call(functools.partial(exchange_kernel, dims), out_shape=[pltpu...  24.7 us
    pallas_call x1, Pallas kernels, on_device(): pl.pallas_call(functools.partial(update_kernel, dims), out_shape=[jax.Sha...  2 us

profile of v2, /device:TPU:32, one launch (start us, length us, event | category | flops | bytes accessed | tf_op | source)
XLA Modules:
  0.0 27.3 jit_solution(990455140012252280)
XLA Ops:
  0.6 0.0 copy-start
  0.6 24.7 %exchange.1 = (f32[64,256]{1,0:T(8,128)S(1)}, bf16[8,64,256]{2,1,0:T(8,128)(2,1)S(1)}, bf16[272,512]{1,0:T(8,128)(2,1)S(1)}, bf16[8,64,128]{2,1,0:T(8,128)(2,1)S(1)}, bf16[272,256]{1,0:T(8,128)(2,1)S(1)}) custom-call(s32[32]{0:T(128)} %live_ref.3, bf16[64,2048]{1,0:T(8,128)(2,1)} %y_hbm.1, bf16[2176,256]{1,0:T(8,128)(2,1)} %a_hbm.1, f32[64,256]{1,0:T(8,128)} %c_hbm.1), custom_call_target="tpu_custom_call" | custom-call | tf_op jit(solution)/shard_map/exchange/pallas_call | solution.py:368
  25.3 0.0 copy-done
  25.3 2.0 %update.1 = (f32[64,256]{1,0:T(8,128)}, bf16[272,256]{1,0:T(8,128)(2,1)}) custom-call(s32[32]{0:T(128)S(1)} %copy-done, f32[64,256]{1,0:T(8,128)S(1)} %get-tuple-element.7.tr, bf16[8,64,256]{2,1,0:T(8,128)(2,1)S(1)} %get-tuple-element.8.b_all, bf16[272,512]{1,0:T(8,128)(2,1)S(1)} %get-tuple-element.9.yt, bf16[8,64,128]{2,1,0:T(8,128)(2,1)S(1)} %get-tuple-element.10.side, ...), custom_call_target="tpu_custom_call" | custom-call | tf_op jit(solution)/shard_map/update/pallas_call | solution.py:407
Async XLA Ops:
  0.6 24.7 %copy-start = (s32[32]{0:T(128)S(1)}, s32[32]{0:T(128)}, u32[]{:S(2)}) copy-start(s32[32]{0:T(128)} %live_ref.3) | copy-start | bytes 388

commit v3 on v1

v3 whole, which is shorter than its diff:
```python
import functools

import jax
import jax.numpy as jnp
from jax import lax
from jax.experimental import pallas as pl
from jax.experimental.pallas import tpu as pltpu
from jax.sharding import PartitionSpec as P

MESH = pl.DeviceIdType.MESH
F32 = jnp.float32
BF16 = jnp.bfloat16
GROUP = 128
LATE_CROSS = {4: 0, 5: 0, 6: 2, 7: 2}
EARLY_CROSS = 2
LATE_ALONG = 2


def dot(a, b, ca=1, cb=0, precision=None):
    return lax.dot_general(
        a, b, (((ca,), (cb,)), ((), ())), preferred_element_type=F32, precision=precision
    )


def halves(x):
    high = x.astype(BF16)
    return high, (x - high.astype(F32)).astype(BF16)


def remote(src, dst, sems, index, **device):
    return pltpu.make_async_remote_copy(
        src_ref=src,
        dst_ref=dst,
        send_sem=sems[0].at[index[0]],
        recv_sem=sems[1].at[index[1]],
        device_id=device,
        device_id_type=MESH,
    )


def exchange_kernel(
    dims,
    live_hbm, y_hbm, a_hbm, c_hbm,
    tr_out, b_all, yt_out, side_out, share_out,
    live_ref, yv, av, cv, y_send, y_recv, rim_in, head_out, tail_out, head_in, tail_in,
    side_head, side_tail,
    load_sem, y_ss, y_rs, b_ss, b_rs, h_ss, h_rs, s_ss, s_rs, ready, side_ready,
):
    slabs, parts, frames, voxels, rows, neurons = dims
    rim = rows - voxels
    share = rows // parts
    wide = share // 128 * 128
    rest = share - wide
    s = lax.axis_index("slab")
    t = lax.axis_index("tm")
    has_next = s < slabs - 1
    has_prev = s > 0
    first, last = t == 0, t == parts - 1
    early = lax.rem(t, 2) == 0
    late = jnp.logical_not(early)

    loads = [
        pltpu.make_async_copy(live_hbm, live_ref, load_sem.at[5]),
        pltpu.make_async_copy(c_hbm, cv, load_sem.at[0]),
        pltpu.make_async_copy(a_hbm.at[:rim], av.at[:rim], load_sem.at[1]),
        pltpu.make_async_copy(a_hbm.at[voxels:], av.at[voxels:], load_sem.at[2]),
        pltpu.make_async_copy(y_hbm, yv, load_sem.at[3]),
        pltpu.make_async_copy(a_hbm.at[rim:voxels], av.at[rim:voxels], load_sem.at[4]),
    ]
    barrier = pltpu.get_barrier_semaphore()

    def greet(**device):
        pl.semaphore_signal(barrier, inc=1, device_id=device, device_id_type=MESH)

    half = parts // 2
    across = t + 1 - 2 * lax.rem(t, 2)
    along = [lax.rem(t + 2 * k, parts) for k in range(1, half)]
    beyond = [across] + [lax.rem(across + 2 * k, parts) for k in range(1, half)]

    @pl.when(has_next)
    def _():
        greet(slab=s + 1)

    @pl.when(has_prev)
    def _():
        greet(slab=s - 1)

    for to in along:
        greet(tm=to)

    @pl.when(early)
    def _():
        for to in beyond:
            greet(tm=to)

    @pl.when(early & has_prev)
    def _():
        greet(slab=s - 1, tm=t * 0 + parts - 1)

    @pl.when(first & has_prev)
    def _():
        for i in range(1, parts - 1):
            greet(slab=s - 1, tm=t + i)

    for load in loads:
        load.start()

    rim_copy = remote(y_hbm.at[:, :rim], rim_in, (h_ss, h_rs), (0, 0), slab=s - 1)
    head_copy = remote(head_out, head_in, (h_ss, h_rs), (1, 1), slab=s - 1)
    tail_copy = remote(tail_out, tail_in, (h_ss, h_rs), (2, 2), slab=s + 1)

    for load in loads[:5]:
        load.wait()
    live = lax.broadcasted_iota(jnp.int32, (1, neurons), 1) < live_ref[s]
    keep_tail = jnp.where(has_next, 1.0, 0.0).astype(F32)
    start = jnp.where(live, cv[...], 0.0)
    c_high, c_low = halves(start)
    head = av[:rim]
    tail = (av[voxels:].astype(F32) * keep_tail).astype(BF16)
    av[voxels:] = tail
    head_out[...] = dot(c_high, head, 1, 1) + dot(c_low, head, 1, 1) - yv[:, :rim].astype(F32)
    tail_out[...] = dot(c_high, tail, 1, 1) + dot(c_low, tail, 1, 1)

    def count(condition, amount=1):
        return jnp.where(condition, jnp.int32(amount), jnp.int32(0))

    heard = half - 1 + count(has_next) + count(has_prev) + count(late, half)
    heard = heard + count(has_next & jnp.logical_not(first)) + count(last & has_next, half - 1)
    pl.semaphore_wait(barrier, heard)

    @pl.when(has_prev)
    def _():
        head_copy.start()

    @pl.when(has_next)
    def _():
        tail_copy.start()

    @pl.when(has_prev)
    def _():
        rim_copy.start()

    @pl.when(late)
    def _():
        for to in beyond:
            pl.semaphore_signal(ready, inc=1, device_id={"tm": to}, device_id_type=MESH)

    @pl.when(last & has_next)
    def _():
        for i in range(1, parts, 2):
            pl.semaphore_signal(
                side_ready, inc=1, device_id={"slab": s + 1, "tm": t - i}, device_id_type=MESH
            )

    y_copies = []

    def pack(p, span):
        base = p * share - p * share // 128 * 128
        for k in range(wide // 128):
            y_send[p, k * frames : (k + 1) * frames] = span[:, base + k * 128 : base + (k + 1) * 128]

    def pack_rest(p, columns):
        pair = jnp.concatenate([columns[: rest // 2], columns[rest // 2 :]], 1)
        y_send[p, wide // 128 * frames :] = pair.astype(BF16)

    group = lax.broadcasted_iota(jnp.int32, (1, 128), 1) // rest
    left = jnp.zeros((frames, 128), F32)
    for p in range(parts - 1):
        tile0 = p * share // 128
        pack(p, yv[:, tile0 * 128 : (tile0 + 3) * 128])
        left = jnp.where(group == p, yv[:, (tile0 + 2) * 128 : (tile0 + 3) * 128].astype(F32), left)
    left_t = left.T
    for p in range(parts - 1):
        pack_rest(p, left_t[p * rest : (p + 1) * rest])

    routes = list(enumerate(beyond, half)) + list(enumerate(along, 1))
    for i, to in routes:
        copy = remote(y_send.at[to], y_recv.at[i], (y_ss, y_rs), (i, i), tm=to)
        y_copies.append((i, to, copy))

    def send_shares(stage):
        for i, to, copy in y_copies:
            crossing = i >= half
            due = jnp.where(late, LATE_CROSS[i], EARLY_CROSS) if crossing else jnp.where(late, LATE_ALONG, 0)
            due = jnp.where(to == parts - 1, jnp.maximum(due, 2), due)

            @pl.when(due == stage)
            def _(copy=copy):
                copy.start()

    send_shares(0)

    loads[5].wait()
    foot = av[...]
    gram = dot(foot, foot, 0, 0)
    eye = lax.broadcasted_iota(jnp.int32, (neurons, neurons), 0) == lax.broadcasted_iota(
        jnp.int32, (neurons, neurons), 1
    )
    scale = jnp.sum(jnp.where(eye, gram, 0.0), 0, keepdims=True) + 1e-6
    own_drive = dot(yv[...], av[:voxels])
    coupled = dot(start, gram, precision=lax.Precision.HIGHEST)
    base = own_drive - coupled

    @pl.when(has_next)
    def _():
        head_copy.wait_recv()

    @pl.when(has_prev)
    def _():
        tail_copy.wait_recv()

    @pl.when(jnp.logical_not(has_next))
    def _():
        head_in[...] = jnp.zeros_like(head_in)

    @pl.when(jnp.logical_not(has_prev))
    def _():
        tail_in[...] = jnp.zeros_like(tail_in)

    nh, nl = halves(head_in[...])
    ph, pw = halves(tail_in[...])
    outside = dot(
        jnp.concatenate([nh, nl, ph, pw], 1), jnp.concatenate([tail, tail, head, head], 0)
    )
    base = base - outside
    done = []
    for g in range(neurons // GROUP):
        cut = slice(g * GROUP, (g + 1) * GROUP)
        change = base[:, cut]
        for h in range(g):
            moved = done[h] - start[:, h * GROUP : (h + 1) * GROUP]
            change = change - dot(
                moved, gram[h * GROUP : (h + 1) * GROUP, cut], precision=lax.Precision.HIGHEST
            )
        done.append(
            jnp.where(
                live[:, cut], jnp.maximum(start[:, cut] + change / scale[:, cut], 0.0), 0.0
            )
        )
    new_tr = jnp.concatenate(done, 1)
    rounded = new_tr.astype(BF16)
    b_all[0] = rounded

    b_cross = remote(b_all.at[0], b_all.at[half], (b_ss, b_rs), (half, half), tm=across)

    @pl.when(late)
    def _():
        b_cross.start()

    def slot_at(x_to, z_to):
        away = lax.rem(x_to - t // 2 + parts, half)
        return jnp.where(lax.rem(t, 2) == z_to, away, half + away)

    to_first = slot_at(0, 0)
    tail_side = remote(
        side_tail, side_out.at[to_first], (s_ss, s_rs), (0, to_first), slab=s + 1, tm=t * 0
    )
    to_last = slot_at(half - 1, 1)
    head_side = remote(
        side_head.at[0], side_out.at[to_last], (s_ss, s_rs), (1, to_last), slab=s - 1, tm=t * 0 + parts - 1
    )
    late_side = remote(
        side_head.at[pl.ds(1, half)], side_out.at[pl.ds(0, half)], (s_ss, s_rs), (2, parts), slab=s - 1
    )
    side_tail[...] = dot(rounded, tail, 1, 1).astype(BF16)

    @pl.when(has_next)
    def _():
        tail_side.start()

    b_copies = []
    for k, to in enumerate(along, 1):
        copy = remote(b_all.at[0], b_all.at[k], (b_ss, b_rs), (k, k), tm=to)
        copy.start()
        b_copies.append(copy)

    @pl.when(has_next)
    def _():
        rim_copy.wait_recv()

    @pl.when(jnp.logical_not(has_next))
    def _():
        rim_in[...] = jnp.zeros_like(rim_in)

    rim_y = rim_in[...]
    p = parts - 1
    tile0 = p * share // 128
    span = jnp.concatenate([yv[:, tile0 * 128 :], rim_y], 1)
    pack(p, span)
    pack_rest(p, rim_y.astype(F32).T[p * rest :])
    @pl.when(early)
    def _():
        pl.semaphore_wait(ready, half)
        b_cross.start()

    send_shares(2)
    tr_out[...] = new_tr

    @pl.when(last & has_prev)
    def _():
        for copy in b_copies:
            copy.wait_recv()
        odd = b_all[:half].reshape(half * frames, neurons)
        side_head[1:] = dot(odd, av[:rim], 1, 1).astype(BF16).reshape(half, frames, rim)
        late_side.start()

    @pl.when(jnp.logical_not(last & has_prev))
    def _():
        side_head[0] = dot(rounded, head, 1, 1).astype(BF16)

    b_cross.wait_recv()
    passed = []
    for k, to in enumerate(along, 1):
        copy = remote(b_all.at[half], b_all.at[half + k], (b_ss, b_rs), (half + k, half + k), tm=to)
        copy.start()
        passed.append(copy)

    @pl.when(early & has_prev)
    def _():
        pl.semaphore_wait(side_ready, 1)
        head_side.start()

    send_shares(3)
    row0 = pl.multiple_of(t * share, 16)
    row = row0 + lax.broadcasted_iota(jnp.int32, (share, 1), 0)
    mine = av[pl.ds(row0, share)].astype(F32)
    share_out[...] = jnp.where(live & (row < rows), mine, 0.0).astype(BF16)

    y_recv[0] = y_send[t]
    for _, _, copy in y_copies:
        copy.wait_recv()
    per = wide // 128
    for k in range(per):
        block = y_recv[:, k * frames : (k + 1) * frames].reshape(parts * frames, 128)
        yt_out[k * 128 : (k + 1) * 128] = block.T
    pairs = [y_recv[i, per * frames :].astype(F32) for i in range(parts)]
    yt_out[wide:] = jnp.concatenate(
        [jnp.concatenate([q[:, :frames] for q in pairs], 1), jnp.concatenate([q[:, frames:] for q in pairs], 1)], 0
    ).astype(BF16)

    @pl.when(jnp.logical_not(last & has_prev))
    def _():
        for copy in b_copies:
            copy.wait_recv()

    for copy in passed:
        copy.wait_recv()

    @pl.when(first & has_prev)
    def _():
        for i in range(parts):
            remote(side_tail, side_out.at[i], (s_ss, s_rs), (0, i), slab=s).wait_recv()

    @pl.when(last & has_next)
    def _():
        late_side.wait_recv()
        for i in range(half, parts):
            remote(side_tail, side_out.at[i], (s_ss, s_rs), (0, i), slab=s).wait_recv()

    for _, _, copy in y_copies:
        copy.wait_send()
    b_cross.wait_send()
    for copy in b_copies + passed:
        copy.wait_send()

    @pl.when(has_prev)
    def _():
        rim_copy.wait_send()
        head_copy.wait_send()

    @pl.when(early & has_prev)
    def _():
        head_side.wait_send()

    @pl.when(last & has_prev)
    def _():
        late_side.wait_send()

    @pl.when(has_next)
    def _():
        tail_copy.wait_send()
        tail_side.wait_send()


def update_kernel(dims, tr, b_all, yt, side, mine, tr_hbm, foot_out, delta, sem):
    slabs, parts, frames, voxels, rows, neurons = dims
    rim = rows - voxels
    share = rows // parts
    s = lax.axis_index("slab")
    t = lax.axis_index("tm")
    store = pltpu.make_async_copy(tr, tr_hbm, sem)
    store.start()
    own = b_all[...].reshape(parts * frames, neurons)
    q = dot(own, own, 0, 0)
    delta[...] = dot(yt[...], own)

    @pl.when((t == 0) & (s > 0))
    def _():
        delta[:rim] = delta[:rim] - dot(side[...].reshape(parts * frames, rim), own, 0, 0)

    @pl.when((t == parts - 1) & (s < slabs - 1))
    def _():
        delta[share - rim :] = delta[share - rim :] - dot(
            side[...].reshape(parts * frames, rim), own, 0, 0
        )

    eye = lax.broadcasted_iota(jnp.int32, (neurons, neurons), 0) == lax.broadcasted_iota(
        jnp.int32, (neurons, neurons), 1
    )
    scale = jnp.maximum(jnp.sum(jnp.where(eye, q, 0.0), 0, keepdims=True), 1.0)
    q_high, q_low = halves(q)
    base = mine[...]
    coupling = dot(base, q_high) + dot(base, q_low)
    foot_out[...] = jnp.maximum(base.astype(F32) + (delta[...] - coupling) / scale, 0.0).astype(
        BF16
    )
    store.wait()


def solution(mesh):
    slabs, parts = mesh.shape["slab"], mesh.shape["tm"]

    def on_device(recording, footprints, traces, live_count):
        frames, voxels = recording.shape
        rows, neurons = footprints.shape
        rim = rows - voxels
        share = rows // parts
        half = parts // 2
        dims = (slabs, parts, frames, voxels, rows, neurons)
        hbm = pl.BlockSpec(memory_space=pltpu.HBM)
        vmem = pl.BlockSpec(memory_space=pltpu.VMEM)
        packed = share // 128 * frames + share % 128 // 2
        dma = pltpu.SemaphoreType.DMA
        tr, b_all, yt, side, mine = pl.pallas_call(
            functools.partial(exchange_kernel, dims),
            out_shape=[
                pltpu.VMEM((frames, neurons), F32),
                pltpu.VMEM((parts, frames, neurons), BF16),
                pltpu.VMEM((share, parts * frames), BF16),
                pltpu.VMEM((parts, frames, rim), BF16),
                pltpu.VMEM((share, neurons), BF16),
            ],
            in_specs=[hbm, hbm, hbm, hbm],
            out_specs=[vmem] * 5,
            scratch_shapes=[
                pltpu.SMEM((slabs,), jnp.int32),
                pltpu.VMEM((frames, voxels), BF16),
                pltpu.VMEM((rows, neurons), BF16),
                pltpu.VMEM((frames, neurons), F32),
                pltpu.VMEM((parts, packed, 128), BF16),
                pltpu.VMEM((parts, packed, 128), BF16),
                pltpu.VMEM((frames, rim), BF16),
                pltpu.VMEM((frames, rim), F32),
                pltpu.VMEM((frames, rim), F32),
                pltpu.VMEM((frames, rim), F32),
                pltpu.VMEM((frames, rim), F32),
                pltpu.VMEM((half + 1, frames, rim), BF16),
                pltpu.VMEM((frames, rim), BF16),
                dma((6,)),
                dma((parts,)),
                dma((parts,)),
                dma((parts,)),
                dma((parts,)),
                dma((3,)),
                dma((3,)),
                dma((3,)),
                dma((parts + 1,)),
                pltpu.SemaphoreType.REGULAR,
                pltpu.SemaphoreType.REGULAR,
            ],
            compiler_params=pltpu.CompilerParams(
                collective_id=0, has_side_effects=True, vmem_limit_bytes=60 * 2**20
            ),
            name="exchange",
        )(live_count, recording, footprints, traces)
        return pl.pallas_call(
            functools.partial(update_kernel, dims),
            out_shape=[
                jax.ShapeDtypeStruct((frames, neurons), F32),
                jax.ShapeDtypeStruct((share, neurons), BF16),
            ],
            in_specs=[vmem] * 5,
            out_specs=[hbm, vmem],
            scratch_shapes=[pltpu.VMEM((share, neurons), F32), dma],
            compiler_params=pltpu.CompilerParams(vmem_limit_bytes=32 * 2**20),
            name="update",
        )(tr, b_all, yt, side, mine)

    placed = (P("tm", "slab"), P(None, "slab"), P("tm", "slab"), P())
    return jax.shard_map(
        on_device,
        mesh=mesh,
        in_specs=placed,
        out_specs=(P("tm", "slab"), P("tm", "slab")),
        check_vma=False,
    )
```

time: 34.9 us -> 25 us (0.72)
  Pallas kernels: 30.4 us -> 24.2 us
  local copies, waits for them, and re-layouts: 3.68 us -> 0 us
    pallas_call x1, Pallas kernels: 28.4 us -> 22.8 us  [on_device(): pl.pallas_call(functools.partial(exchange_kernel, dims), out_shape=[pltpu...]
    unnamed x8 -> x0, local copies, waits for them, and re-layouts: 3.68 us -> none
    pallas_call x1, Pallas kernels: 2 us -> 1.46 us  [on_device(): pl.pallas_call(functools.partial(update_kernel, dims), out_shape=[jax.Sha...]
where the time goes in v3:
time: 25 us; the launch traced here: 24.9 us
  Pallas kernels  24.2 us (97%)
  between operations  0.64 us (3%)
    pallas_call x1, Pallas kernels, on_device(): pl.pallas_call(functools.partial(exchange_kernel, dims), out_shape=[pltpu...  22.8 us
    pallas_call x1, Pallas kernels, on_device(): pl.pallas_call(functools.partial(update_kernel, dims), out_shape=[jax.Sha...  1.46 us

profile of v3, /device:TPU:32, one launch (start us, length us, event | category | flops | bytes accessed | tf_op | source)
XLA Modules:
  0.0 24.9 jit_solution(13529140628307355307)
XLA Ops:
  0.6 22.8 %exchange.1 = (f32[64,256]{1,0:T(8,128)S(1)}, bf16[8,64,256]{2,1,0:T(8,128)(2,1)S(1)}, bf16[272,512]{1,0:T(8,128)(2,1)S(1)}, bf16[8,64,128]{2,1,0:T(8,128)(2,1)S(1)}, bf16[272,256]{1,0:T(8,128)(2,1)S(1)}) custom-call(s32[32]{0:T(128)} %live_hbm.1, bf16[64,2048]{1,0:T(8,128)(2,1)} %y_hbm.1, bf16[2176,256]{1,0:T(8,128)(2,1)} %a_hbm.1, f32[64,256]{1,0:T(8,128)} %c_hbm.1), custom_call_target="tpu_custom_call" | custom-call | tf_op jit(solution)/shard_map/exchange/pallas_call | solution.py:434
  23.4 1.5 %update.1 = (f32[64,256]{1,0:T(8,128)}, bf16[272,256]{1,0:T(8,128)(2,1)}) custom-call(f32[64,256]{1,0:T(8,128)S(1)} %get-tuple-element.7.tr, bf16[8,64,256]{2,1,0:T(8,128)(2,1)S(1)} %get-tuple-element.8.b_all, bf16[272,512]{1,0:T(8,128)(2,1)S(1)} %get-tuple-element.9.yt, bf16[8,64,128]{2,1,0:T(8,128)(2,1)S(1)} %get-tuple-element.10.side, ...), custom_call_target="tpu_custom_call" | custom-call | tf_op jit(solution)/shard_map/update/pallas_call | solution.py:476

commit v4 on v3

--- a/solution.py
+++ b/solution.py
@@ -11,7 +11,7 @@
 F32 = jnp.float32
 BF16 = jnp.bfloat16
 GROUP = 128
-LATE_CROSS = {4: 0, 5: 0, 6: 2, 7: 2}
+LATE_CROSS = ((0, 0, 2, 2), (0, 0, 0, 2), (0, 0, 0, 2), (0, 2, 2, 2))
 EARLY_CROSS = 2
 LATE_ALONG = 2
 
@@ -41,7 +41,7 @@
 def exchange_kernel(
     dims,
     live_hbm, y_hbm, a_hbm, c_hbm,
-    tr_out, b_all, yt_out, side_out, share_out,
+    tr_out, b_all, yt_out, side_out, share_out, q_part, m_part,
     live_ref, yv, av, cv, y_send, y_recv, rim_in, head_out, tail_out, head_in, tail_in,
     side_head, side_tail,
     load_sem, y_ss, y_rs, b_ss, b_rs, h_ss, h_rs, s_ss, s_rs, ready, side_ready,
@@ -181,7 +181,13 @@
     def send_shares(stage):
         for i, to, copy in y_copies:
             crossing = i >= half
-            due = jnp.where(late, LATE_CROSS[i], EARLY_CROSS) if crossing else jnp.where(late, LATE_ALONG, 0)
+            if crossing:
+                due = jnp.int32(LATE_CROSS[0][i - half])
+                for zone, stages in enumerate(LATE_CROSS):
+                    due = jnp.where(s * len(LATE_CROSS) // slabs == zone, stages[i - half], due)
+                due = jnp.where(late, jnp.where(to == 0, 0, due), EARLY_CROSS)
+            else:
+                due = jnp.where(late, LATE_ALONG, 0)
             due = jnp.where(to == parts - 1, jnp.maximum(due, 2), due)
 
             @pl.when(due == stage)
@@ -326,34 +332,54 @@
     mine = av[pl.ds(row0, share)].astype(F32)
     share_out[...] = jnp.where(live & (row < rows), mine, 0.0).astype(BF16)
 
+    per = wide // 128
+
+    def voxels_first(base):
+        tiles = [
+            y_recv[base : base + half, k * frames : (k + 1) * frames].reshape(half * frames, 128).T
+            for k in range(per)
+        ]
+        pairs = [y_recv[base + i, per * frames :].astype(F32) for i in range(half)]
+        low = jnp.concatenate([q[:, :frames] for q in pairs], 1)
+        high = jnp.concatenate([q[:, frames:] for q in pairs], 1)
+        return jnp.concatenate(tiles + [jnp.concatenate([low, high], 0).astype(BF16)], 0)
+
     y_recv[0] = y_send[t]
-    for _, _, copy in y_copies:
-        copy.wait_recv()
-    per = wide // 128
-    for k in range(per):
-        block = y_recv[:, k * frames : (k + 1) * frames].reshape(parts * frames, 128)
-        yt_out[k * 128 : (k + 1) * 128] = block.T
-    pairs = [y_recv[i, per * frames :].astype(F32) for i in range(parts)]
-    yt_out[wide:] = jnp.concatenate(
-        [jnp.concatenate([q[:, :frames] for q in pairs], 1), jnp.concatenate([q[:, frames:] for q in pairs], 1)], 0
-    ).astype(BF16)
+    for i, _, copy in y_copies:
+        if i < half:
+            copy.wait_recv()
 
     @pl.when(jnp.logical_not(last & has_prev))
     def _():
         for copy in b_copies:
             copy.wait_recv()
 
+    near = b_all[:half].reshape(half * frames, neurons)
+    q_part[...] = dot(near, near, 0, 0)
+    m_part[...] = dot(voxels_first(0), near)
+
+    @pl.when(first & has_prev)
+    def _():
+        for i in range(half):
+            remote(side_tail, side_out.at[i], (s_ss, s_rs), (0, i), slab=s).wait_recv()
+        sides = side_out[:half].reshape(half * frames, rim)
+        m_part[:rim] = m_part[:rim] - dot(sides, near, 0, 0)
+
+    @pl.when(last & has_next)
+    def _():
+        late_side.wait_recv()
+        sides = side_out[:half].reshape(half * frames, rim)
+        m_part[share - rim :] = m_part[share - rim :] - dot(sides, near, 0, 0)
+
+    for i, _, copy in y_copies:
+        if i >= half:
+            copy.wait_recv()
+    yt_out[...] = voxels_first(half)
     for copy in passed:
         copy.wait_recv()
 
-    @pl.when(first & has_prev)
-    def _():
-        for i in range(parts):
-            remote(side_tail, side_out.at[i], (s_ss, s_rs), (0, i), slab=s).wait_recv()
-
-    @pl.when(last & has_next)
-    def _():
-        late_side.wait_recv()
+    @pl.when((first & has_prev) | (last & has_next))
+    def _():
         for i in range(half, parts):
             remote(side_tail, side_out.at[i], (s_ss, s_rs), (0, i), slab=s).wait_recv()
 
@@ -382,26 +408,27 @@
         tail_side.wait_send()
 
 
-def update_kernel(dims, tr, b_all, yt, side, mine, tr_hbm, foot_out, delta, sem):
+def update_kernel(dims, tr, b_all, yt, side, mine, q_part, m_part, tr_hbm, foot_hbm, delta, foot, sems):
     slabs, parts, frames, voxels, rows, neurons = dims
     rim = rows - voxels
     share = rows // parts
+    half = parts // 2
     s = lax.axis_index("slab")
     t = lax.axis_index("tm")
-    store = pltpu.make_async_copy(tr, tr_hbm, sem)
-    store.start()
-    own = b_all[...].reshape(parts * frames, neurons)
-    q = dot(own, own, 0, 0)
-    delta[...] = dot(yt[...], own)
+    stores = [pltpu.make_async_copy(tr, tr_hbm, sems.at[0])]
+    stores[0].start()
+    far = b_all[half:].reshape(half * frames, neurons)
+    q = q_part[...] + dot(far, far, 0, 0)
+    delta[...] = m_part[...] + dot(yt[...], far)
 
     @pl.when((t == 0) & (s > 0))
     def _():
-        delta[:rim] = delta[:rim] - dot(side[...].reshape(parts * frames, rim), own, 0, 0)
+        delta[:rim] = delta[:rim] - dot(side[half:].reshape(half * frames, rim), far, 0, 0)
 
     @pl.when((t == parts - 1) & (s < slabs - 1))
     def _():
         delta[share - rim :] = delta[share - rim :] - dot(
-            side[...].reshape(parts * frames, rim), own, 0, 0
+            side[half:].reshape(half * frames, rim), far, 0, 0
         )
 
     eye = lax.broadcasted_iota(jnp.int32, (neurons, neurons), 0) == lax.broadcasted_iota(
@@ -409,12 +436,18 @@
     )
     scale = jnp.maximum(jnp.sum(jnp.where(eye, q, 0.0), 0, keepdims=True), 1.0)
     q_high, q_low = halves(q)
-    base = mine[...]
-    coupling = dot(base, q_high) + dot(base, q_low)
-    foot_out[...] = jnp.maximum(base.astype(F32) + (delta[...] - coupling) / scale, 0.0).astype(
-        BF16
-    )
-    store.wait()
+    cut = share // 32 * 16
+    for n, span in enumerate((slice(0, cut), slice(cut, share))):
+        base = mine[span]
+        coupling = dot(base, q_high) + dot(base, q_low)
+        foot[span] = jnp.maximum(
+            base.astype(F32) + (delta[span] - coupling) / scale, 0.0
+        ).astype(BF16)
+        store = pltpu.make_async_copy(foot.at[span], foot_hbm.at[span], sems.at[1 + n])
+        store.start()
+        stores.append(store)
+    for store in stores:
+        store.wait()
 
 
 def solution(mesh):
@@ -431,17 +464,19 @@
         vmem = pl.BlockSpec(memory_space=pltpu.VMEM)
         packed = share // 128 * frames + share % 128 // 2
         dma = pltpu.SemaphoreType.DMA
-        tr, b_all, yt, side, mine = pl.pallas_call(
+        tr, b_all, yt, side, mine, q_part, m_part = pl.pallas_call(
             functools.partial(exchange_kernel, dims),
             out_shape=[
                 pltpu.VMEM((frames, neurons), F32),
                 pltpu.VMEM((parts, frames, neurons), BF16),
-                pltpu.VMEM((share, parts * frames), BF16),
+                pltpu.VMEM((share, half * frames), BF16),
                 pltpu.VMEM((parts, frames, rim), BF16),
                 pltpu.VMEM((share, neurons), BF16),
+                pltpu.VMEM((neurons, neurons), F32),
+                pltpu.VMEM((share, neurons), F32),
             ],
             in_specs=[hbm, hbm, hbm, hbm],
-            out_specs=[vmem] * 5,
+            out_specs=[vmem] * 7,
             scratch_shapes=[
                 pltpu.SMEM((slabs,), jnp.int32),
                 pltpu.VMEM((frames, voxels), BF16),
@@ -479,12 +514,16 @@
                 jax.ShapeDtypeStruct((frames, neurons), F32),
                 jax.ShapeDtypeStruct((share, neurons), BF16),
             ],
-            in_specs=[vmem] * 5,
-            out_specs=[hbm, vmem],
-            scratch_shapes=[pltpu.VMEM((share, neurons), F32), dma],
+            in_specs=[vmem] * 7,
+            out_specs=[hbm, hbm],
+            scratch_shapes=[
+                pltpu.VMEM((share, neurons), F32),
+                pltpu.VMEM((share, neurons), BF16),
+                dma((3,)),
+            ],
             compiler_params=pltpu.CompilerParams(vmem_limit_bytes=32 * 2**20),
             name="update",
-        )(tr, b_all, yt, side, mine)
+        )(tr, b_all, yt, side, mine, q_part, m_part)
 
     placed = (P("tm", "slab"), P(None, "slab"), P("tm", "slab"), P())
     return jax.shard_map(

time: 25 us -> 24.6 us (0.984)
  Pallas kernels: 24.2 us -> 23.9 us
    pallas_call x1, Pallas kernels: 22.8 us -> 22.5 us  [on_device(): pl.pallas_call(functools.partial(exchange_kernel, dims), out_shape=[pltpu...]
where the time goes in v4:
time: 24.6 us; the launch traced here: 24.5 us
  Pallas kernels  23.9 us (97%)
  between operations  0.64 us (3%)
    pallas_call x1, Pallas kernels, on_device(): pl.pallas_call(functools.partial(exchange_kernel, dims), out_shape=[pltpu...  22.5 us
    pallas_call x1, Pallas kernels, on_device(): pl.pallas_call(functools.partial(update_kernel, dims), out_shape=[jax.Sha...  1.38 us

profile of v4, /device:TPU:32, one launch (start us, length us, event | category | flops | bytes accessed | tf_op | source)
XLA Modules:
  0.0 24.5 jit_solution(8895129448597301726)
XLA Ops:
  0.6 22.5 %exchange.1 = (f32[64,256]{1,0:T(8,128)S(1)}, bf16[8,64,256]{2,1,0:T(8,128)(2,1)S(1)}, bf16[272,256]{1,0:T(8,128)(2,1)S(1)}, bf16[8,64,128]{2,1,0:T(8,128)(2,1)S...) custom-call(s32[32]{0:T(128)} %live_hbm.1, bf16[64,2048]{1,0:T(8,128)(2,1)} %y_hbm.1, ...), custom_call_target="tpu_custom_call" | custom-call | tf_op jit(solution)/shard_map/exchange/pallas_call | solution.py:467
  23.1 1.4 %update.1 = (f32[64,256]{1,0:T(8,128)}, bf16[272,256]{1,0:T(8,128)(2,1)}) custom-call(f32[64,256]{1,0:T(8,128)S(1)} %get-tuple-element.9.tr, bf16[8,64,256]{2,1,0:T(8,128)(2,1)S(1)} %get-tuple-element.10.b_all, bf16[272,256]{1,0:T(8,128)(2,1)S(1)} %get-tuple-element.11.yt, bf16[8,64,128]{2,1,0:T(8,128)(2,1)S(1)} %get-tuple-element.12.side, ...), custom_call_target="tpu_custom_call" | custom-call | tf_op jit(solution)/shard_map/update/pallas_call | solution.py:511

commit v5 on v4

--- a/solution.py
+++ b/solution.py
@@ -13,7 +13,7 @@
 GROUP = 128
 LATE_CROSS = ((0, 0, 2, 2), (0, 0, 0, 2), (0, 0, 0, 2), (0, 2, 2, 2))
 EARLY_CROSS = 2
-LATE_ALONG = 2
+PATIENT = 2
 
 
 def dot(a, b, ca=1, cb=0, precision=None):
@@ -58,6 +58,7 @@
     first, last = t == 0, t == parts - 1
     early = lax.rem(t, 2) == 0
     late = jnp.logical_not(early)
+    patient = late & (s * len(LATE_CROSS) // slabs < PATIENT)
 
     loads = [
         pltpu.make_async_copy(live_hbm, live_ref, load_sem.at[5]),
@@ -85,8 +86,10 @@
     def _():
         greet(slab=s - 1)
 
-    for to in along:
-        greet(tm=to)
+    @pl.when(jnp.logical_not(patient))
+    def _():
+        for to in along:
+            greet(tm=to)
 
     @pl.when(early)
     def _():
@@ -121,37 +124,6 @@
     head_out[...] = dot(c_high, head, 1, 1) + dot(c_low, head, 1, 1) - yv[:, :rim].astype(F32)
     tail_out[...] = dot(c_high, tail, 1, 1) + dot(c_low, tail, 1, 1)
 
-    def count(condition, amount=1):
-        return jnp.where(condition, jnp.int32(amount), jnp.int32(0))
-
-    heard = half - 1 + count(has_next) + count(has_prev) + count(late, half)
-    heard = heard + count(has_next & jnp.logical_not(first)) + count(last & has_next, half - 1)
-    pl.semaphore_wait(barrier, heard)
-
-    @pl.when(has_prev)
-    def _():
-        head_copy.start()
-
-    @pl.when(has_next)
-    def _():
-        tail_copy.start()
-
-    @pl.when(has_prev)
-    def _():
-        rim_copy.start()
-
-    @pl.when(late)
-    def _():
-        for to in beyond:
-            pl.semaphore_signal(ready, inc=1, device_id={"tm": to}, device_id_type=MESH)
-
-    @pl.when(last & has_next)
-    def _():
-        for i in range(1, parts, 2):
-            pl.semaphore_signal(
-                side_ready, inc=1, device_id={"slab": s + 1, "tm": t - i}, device_id_type=MESH
-            )
-
     y_copies = []
 
     def pack(p, span):
@@ -173,6 +145,37 @@
     for p in range(parts - 1):
         pack_rest(p, left_t[p * rest : (p + 1) * rest])
 
+    def count(condition, amount=1):
+        return jnp.where(condition, jnp.int32(amount), jnp.int32(0))
+
+    heard = count(has_next) + count(has_prev) + count(late, half) + count(jnp.logical_not(patient), half - 1)
+    heard = heard + count(has_next & jnp.logical_not(first)) + count(last & has_next, half - 1)
+    pl.semaphore_wait(barrier, heard)
+
+    @pl.when(has_prev)
+    def _():
+        head_copy.start()
+
+    @pl.when(has_next)
+    def _():
+        tail_copy.start()
+
+    @pl.when(has_prev)
+    def _():
+        rim_copy.start()
+
+    @pl.when(late)
+    def _():
+        for to in beyond:
+            pl.semaphore_signal(ready, inc=1, device_id={"tm": to}, device_id_type=MESH)
+
+    @pl.when(last & has_next)
+    def _():
+        for i in range(1, parts, 2):
+            pl.semaphore_signal(
+                side_ready, inc=1, device_id={"slab": s + 1, "tm": t - i}, device_id_type=MESH
+            )
+
     routes = list(enumerate(beyond, half)) + list(enumerate(along, 1))
     for i, to in routes:
         copy = remote(y_send.at[to], y_recv.at[i], (y_ss, y_rs), (i, i), tm=to)
@@ -187,7 +190,7 @@
                     due = jnp.where(s * len(LATE_CROSS) // slabs == zone, stages[i - half], due)
                 due = jnp.where(late, jnp.where(to == 0, 0, due), EARLY_CROSS)
             else:
-                due = jnp.where(late, LATE_ALONG, 0)
+                due = jnp.where(patient, 3, jnp.where(late, 2, 0))
             due = jnp.where(to == parts - 1, jnp.maximum(due, 2), due)
 
             @pl.when(due == stage)
@@ -277,8 +280,12 @@
     b_copies = []
     for k, to in enumerate(along, 1):
         copy = remote(b_all.at[0], b_all.at[k], (b_ss, b_rs), (k, k), tm=to)
-        copy.start()
         b_copies.append(copy)
+
+    @pl.when(jnp.logical_not(patient))
+    def _():
+        for copy in b_copies:
+            copy.start()
 
     @pl.when(has_next)
     def _():
@@ -302,6 +309,30 @@
     send_shares(2)
     tr_out[...] = new_tr
 
+    @pl.when(jnp.logical_not(last & has_prev))
+    def _():
+        side_head[0] = dot(rounded, head, 1, 1).astype(BF16)
+
+    b_cross.wait_recv()
+
+    @pl.when(patient)
+    def _():
+        for copy in b_copies:
+            copy.start()
+
+    passed = []
+    for k, to in enumerate(along, 1):
+        copy = remote(b_all.at[half], b_all.at[half + k], (b_ss, b_rs), (half + k, half + k), tm=to)
+        copy.start()
+        passed.append(copy)
+
+    @pl.when(early & has_prev)
+    def _():
+        pl.semaphore_wait(side_ready, 1)
+        head_side.start()
+
+    send_shares(3)
+
     @pl.when(last & has_prev)
     def _():
         for copy in b_copies:
@@ -310,23 +341,6 @@
         side_head[1:] = dot(odd, av[:rim], 1, 1).astype(BF16).reshape(half, frames, rim)
         late_side.start()
 
-    @pl.when(jnp.logical_not(last & has_prev))
-    def _():
-        side_head[0] = dot(rounded, head, 1, 1).astype(BF16)
-
-    b_cross.wait_recv()
-    passed = []
-    for k, to in enumerate(along, 1):
-        copy = remote(b_all.at[half], b_all.at[half + k], (b_ss, b_rs), (half + k, half + k), tm=to)
-        copy.start()
-        passed.append(copy)
-
-    @pl.when(early & has_prev)
-    def _():
-        pl.semaphore_wait(side_ready, 1)
-        head_side.start()
-
-    send_shares(3)
     row0 = pl.multiple_of(t * share, 16)
     row = row0 + lax.broadcasted_iota(jnp.int32, (share, 1), 0)
     mine = av[pl.ds(row0, share)].astype(F32)

time: 24.6 us -> 23.9 us (0.972)
  Pallas kernels: 23.9 us -> 23 us
    pallas_call x1, Pallas kernels: 22.5 us -> 21.7 us  [on_device(): pl.pallas_call(functools.partial(exchange_kernel, dims), out_shape=[pltpu...]
where the time goes in v5:
time: 23.9 us; the launch traced here: 23.7 us
  Pallas kernels  23 us (96%)
  between operations  0.64 us (3%)
    pallas_call x1, Pallas kernels, on_device(): pl.pallas_call(functools.partial(exchange_kernel, dims), out_shape=[pltpu...  21.7 us
    pallas_call x1, Pallas kernels, on_device(): pl.pallas_call(functools.partial(update_kernel, dims), out_shape=[jax.Sha...  1.38 us

profile of v5, /device:TPU:32, one launch (start us, length us, event | category | flops | bytes accessed | tf_op | source)
XLA Modules:
  0.0 23.7 jit_solution(12709409404784235684)
XLA Ops:
  0.6 21.7 %exchange.1 = (f32[64,256]{1,0:T(8,128)S(1)}, bf16[8,64,256]{2,1,0:T(8,128)(2,1)S(1)}, bf16[272,256]{1,0:T(8,128)(2,1)S(1)}, bf16[8,64,128]{2,1,0:T(8,128)(2,1)S...) custom-call(s32[32]{0:T(128)} %live_hbm.1, bf16[64,2048]{1,0:T(8,128)(2,1)} %y_hbm.1, ...), custom_call_target="tpu_custom_call" | custom-call | tf_op jit(solution)/shard_map/exchange/pallas_call | solution.py:481
  22.3 1.4 %update.1 = (f32[64,256]{1,0:T(8,128)}, bf16[272,256]{1,0:T(8,128)(2,1)}) custom-call(f32[64,256]{1,0:T(8,128)S(1)} %get-tuple-element.9.tr, bf16[8,64,256]{2,1,0:T(8,128)(2,1)S(1)} %get-tuple-element.10.b_all, bf16[272,256]{1,0:T(8,128)(2,1)S(1)} %get-tuple-element.11.yt, bf16[8,64,128]{2,1,0:T(8,128)(2,1)S(1)} %get-tuple-element.12.side, ...), custom_call_target="tpu_custom_call" | custom-call | tf_op jit(solution)/shard_map/update/pallas_call | solution.py:525

commit v6 on v5

--- a/solution.py
+++ b/solution.py
@@ -348,12 +348,12 @@
 
     per = wide // 128
 
-    def voxels_first(base):
+    def voxels_first(base, many):
         tiles = [
-            y_recv[base : base + half, k * frames : (k + 1) * frames].reshape(half * frames, 128).T
+            y_recv[base : base + many, k * frames : (k + 1) * frames].reshape(many * frames, 128).T
             for k in range(per)
         ]
-        pairs = [y_recv[base + i, per * frames :].astype(F32) for i in range(half)]
+        pairs = [y_recv[base + i, per * frames :].astype(F32) for i in range(many)]
         low = jnp.concatenate([q[:, :frames] for q in pairs], 1)
         high = jnp.concatenate([q[:, frames:] for q in pairs], 1)
         return jnp.concatenate(tiles + [jnp.concatenate([low, high], 0).astype(BF16)], 0)
@@ -370,7 +370,7 @@
 
     near = b_all[:half].reshape(half * frames, neurons)
     q_part[...] = dot(near, near, 0, 0)
-    m_part[...] = dot(voxels_first(0), near)
+    m_part[...] = dot(voxels_first(0, half), near)
 
     @pl.when(first & has_prev)
     def _():
@@ -385,10 +385,11 @@
         sides = side_out[:half].reshape(half * frames, rim)
         m_part[share - rim :] = m_part[share - rim :] - dot(sides, near, 0, 0)
 
-    for i, _, copy in y_copies:
-        if i >= half:
-            copy.wait_recv()
-    yt_out[...] = voxels_first(half)
+    for n in range(0, half, 2):
+        for i, _, copy in y_copies:
+            if i - half in (n, n + 1):
+                copy.wait_recv()
+        yt_out[:, n * frames : (n + 2) * frames] = voxels_first(half + n, 2)
     for copy in passed:
         copy.wait_recv()
 
@@ -422,7 +423,7 @@
         tail_side.wait_send()
 
 
-def update_kernel(dims, tr, b_all, yt, side, mine, q_part, m_part, tr_hbm, foot_hbm, delta, foot, sems):
+def update_kernel(dims, tr, b_all, yt, side, mine, q_part, m_part, tr_hbm, foot_hbm, foot, sems):
     slabs, parts, frames, voxels, rows, neurons = dims
     rim = rows - voxels
     share = rows // parts
@@ -433,18 +434,11 @@
     stores[0].start()
     far = b_all[half:].reshape(half * frames, neurons)
     q = q_part[...] + dot(far, far, 0, 0)
-    delta[...] = m_part[...] + dot(yt[...], far)
-
-    @pl.when((t == 0) & (s > 0))
-    def _():
-        delta[:rim] = delta[:rim] - dot(side[half:].reshape(half * frames, rim), far, 0, 0)
-
-    @pl.when((t == parts - 1) & (s < slabs - 1))
-    def _():
-        delta[share - rim :] = delta[share - rim :] - dot(
-            side[half:].reshape(half * frames, rim), far, 0, 0
-        )
-
+    sides = dot(side[half:].reshape(half * frames, rim), far, 0, 0)
+    top = jnp.where((t == 0) & (s > 0), sides, 0.0)
+    bottom = jnp.where((t == parts - 1) & (s < slabs - 1), sides, 0.0)
+    middle = jnp.zeros((share - 2 * rim, neurons), F32)
+    delta = m_part[...] + dot(yt[...], far) - jnp.concatenate([top, middle, bottom], 0)
     eye = lax.broadcasted_iota(jnp.int32, (neurons, neurons), 0) == lax.broadcasted_iota(
         jnp.int32, (neurons, neurons), 1
     )
@@ -531,7 +525,6 @@
             in_specs=[vmem] * 7,
             out_specs=[hbm, hbm],
             scratch_shapes=[
-                pltpu.VMEM((share, neurons), F32),
                 pltpu.VMEM((share, neurons), BF16),
                 dma((3,)),
             ],

time: 23.9 us -> 23.6 us (0.987)
  no operation moved by 1% of the time
where the time goes in v6:
time: 23.6 us; the launch traced here: 23.4 us
  Pallas kernels  22.8 us (97%)
  between operations  0.64 us (3%)
    pallas_call x1, Pallas kernels, on_device(): pl.pallas_call(functools.partial(exchange_kernel, dims), out_shape=[pltpu...  21.7 us
    pallas_call x1, Pallas kernels, on_device(): pl.pallas_call(functools.partial(update_kernel, dims), out_shape=[jax.Sha...  1.15 us

profile of v6, /device:TPU:32, one launch (start us, length us, event | category | flops | bytes accessed | tf_op | source)
XLA Modules:
  0.0 23.4 jit_solution(6361848984658296351)
XLA Ops:
  0.6 21.7 %exchange.1 = (f32[64,256]{1,0:T(8,128)S(1)}, bf16[8,64,256]{2,1,0:T(8,128)(2,1)S(1)}, bf16[272,256]{1,0:T(8,128)(2,1)S(1)}, bf16[8,64,128]{2,1,0:T(8,128)(2,1)S...) custom-call(s32[32]{0:T(128)} %live_hbm.1, bf16[64,2048]{1,0:T(8,128)(2,1)} %y_hbm.1, ...), custom_call_target="tpu_custom_call" | custom-call | tf_op jit(solution)/shard_map/exchange/pallas_call | solution.py:475
  22.3 1.2 %update.1 = (f32[64,256]{1,0:T(8,128)}, bf16[272,256]{1,0:T(8,128)(2,1)}) custom-call(f32[64,256]{1,0:T(8,128)S(1)} %get-tuple-element.9.tr, bf16[8,64,256]{2,1,0:T(8,128)(2,1)S(1)} %get-tuple-element.10.b_all, bf16[272,256]{1,0:T(8,128)(2,1)S(1)} %get-tuple-element.11.yt, bf16[8,64,128]{2,1,0:T(8,128)(2,1)S(1)} %get-tuple-element.12.side, ...), custom_call_target="tpu_custom_call" | custom-call | tf_op jit(solution)/shard_map/update/pallas_call | solution.py:519

commit v7 on v6

--- a/solution.py
+++ b/solution.py
@@ -14,6 +14,7 @@
 LATE_CROSS = ((0, 0, 2, 2), (0, 0, 0, 2), (0, 0, 0, 2), (0, 2, 2, 2))
 EARLY_CROSS = 2
 PATIENT = 2
+PIECES = 2
 
 
 def dot(a, b, ca=1, cb=0, precision=None):
@@ -250,11 +251,16 @@
     rounded = new_tr.astype(BF16)
     b_all[0] = rounded
 
-    b_cross = remote(b_all.at[0], b_all.at[half], (b_ss, b_rs), (half, half), tm=across)
+    pieces = [(n * parts, pl.ds(n * frames // PIECES, frames // PIECES)) for n in range(PIECES)]
+    b_cross = [
+        remote(b_all.at[0, span], b_all.at[half, span], (b_ss, b_rs), (n + half, n + half), tm=across)
+        for n, span in pieces
+    ]
 
     @pl.when(late)
     def _():
-        b_cross.start()
+        for copy in b_cross:
+            copy.start()
 
     def slot_at(x_to, z_to):
         away = lax.rem(x_to - t // 2 + parts, half)
@@ -304,7 +310,8 @@
     @pl.when(early)
     def _():
         pl.semaphore_wait(ready, half)
-        b_cross.start()
+        for copy in b_cross:
+            copy.start()
 
     send_shares(2)
     tr_out[...] = new_tr
@@ -313,18 +320,23 @@
     def _():
         side_head[0] = dot(rounded, head, 1, 1).astype(BF16)
 
-    b_cross.wait_recv()
-
-    @pl.when(patient)
-    def _():
-        for copy in b_copies:
+    passed = []
+    for (n, span), crossed in zip(pieces, b_cross):
+        crossed.wait_recv()
+        if n == 0:
+
+            @pl.when(patient)
+            def _():
+                for copy in b_copies:
+                    copy.start()
+
+        for k, to in enumerate(along, 1):
+            slot = half + k
+            copy = remote(
+                b_all.at[half, span], b_all.at[slot, span], (b_ss, b_rs), (n + slot, n + slot), tm=to
+            )
             copy.start()
-
-    passed = []
-    for k, to in enumerate(along, 1):
-        copy = remote(b_all.at[half], b_all.at[half + k], (b_ss, b_rs), (half + k, half + k), tm=to)
-        copy.start()
-        passed.append(copy)
+            passed.append(copy)
 
     @pl.when(early & has_prev)
     def _():
@@ -400,8 +412,7 @@
 
     for _, _, copy in y_copies:
         copy.wait_send()
-    b_cross.wait_send()
-    for copy in b_copies + passed:
+    for copy in b_cross + b_copies + passed:
         copy.wait_send()
 
     @pl.when(has_prev)
@@ -502,8 +513,8 @@
                 dma((6,)),
                 dma((parts,)),
                 dma((parts,)),
-                dma((parts,)),
-                dma((parts,)),
+                dma((PIECES * parts,)),
+                dma((PIECES * parts,)),
                 dma((3,)),
                 dma((3,)),
                 dma((3,)),

time: 23.6 us -> 23.7 us (level)
  no operation moved by 1% of the time
where the time goes in v7:
time: 23.7 us; the launch traced here: 23.6 us
  Pallas kernels  23 us (97%)
  between operations  0.64 us (3%)
    pallas_call x1, Pallas kernels, on_device(): pl.pallas_call(functools.partial(exchange_kernel, dims), out_shape=[pltpu...  21.8 us
    pallas_call x1, Pallas kernels, on_device(): pl.pallas_call(functools.partial(update_kernel, dims), out_shape=[jax.Sha...  1.15 us

profile of v7, /device:TPU:32, one launch (start us, length us, event | category | flops | bytes accessed | tf_op | source)
XLA Modules:
  0.0 23.6 jit_solution(8577916872916553473)
XLA Ops:
  0.6 21.8 %exchange.1 = (f32[64,256]{1,0:T(8,128)S(1)}, bf16[8,64,256]{2,1,0:T(8,128)(2,1)S(1)}, bf16[272,256]{1,0:T(8,128)(2,1)S(1)}, bf16[8,64,128]{2,1,0:T(8,128)(2,1)S...) custom-call(s32[32]{0:T(128)} %live_hbm.1, bf16[64,2048]{1,0:T(8,128)(2,1)} %y_hbm.1, ...), custom_call_target="tpu_custom_call" | custom-call | tf_op jit(solution)/shard_map/exchange/pallas_call | solution.py:486
  22.4 1.2 %update.1 = (f32[64,256]{1,0:T(8,128)}, bf16[272,256]{1,0:T(8,128)(2,1)}) custom-call(f32[64,256]{1,0:T(8,128)S(1)} %get-tuple-element.9.tr, bf16[8,64,256]{2,1,0:T(8,128)(2,1)S(1)} %get-tuple-element.10.b_all, bf16[272,256]{1,0:T(8,128)(2,1)S(1)} %get-tuple-element.11.yt, bf16[8,64,128]{2,1,0:T(8,128)(2,1)S(1)} %get-tuple-element.12.side, ...), custom_call_target="tpu_custom_call" | custom-call | tf_op jit(solution)/shard_map/update/pallas_call | solution.py:530

commit v8 on v7

--- a/solution.py
+++ b/solution.py
@@ -11,7 +11,7 @@
 F32 = jnp.float32
 BF16 = jnp.bfloat16
 GROUP = 128
-LATE_CROSS = ((0, 0, 2, 2), (0, 0, 0, 2), (0, 0, 0, 2), (0, 2, 2, 2))
+LATE_CROSS = ((0, 2, 2, 2), (0, 0, 0, 2), (0, 0, 2, 2), (0, 2, 2, 2))
 EARLY_CROSS = 2
 PATIENT = 2
 PIECES = 2

time: 23.7 us -> 23.7 us (level)
  no operation moved by 1% of the time
where the time goes in v8:
time: 23.7 us; the launch traced here: 23.6 us
  Pallas kernels  23 us (97%)
  between operations  0.64 us (3%)
    pallas_call x1, Pallas kernels, on_device(): pl.pallas_call(functools.partial(exchange_kernel, dims), out_shape=[pltpu...  21.8 us
    pallas_call x1, Pallas kernels, on_device(): pl.pallas_call(functools.partial(update_kernel, dims), out_shape=[jax.Sha...  1.15 us

profile of v8, /device:TPU:32, one launch (start us, length us, event | category | flops | bytes accessed | tf_op | source)
XLA Modules:
  0.0 23.6 jit_solution(12098947648670380060)
XLA Ops:
  0.6 21.8 %exchange.1 = (f32[64,256]{1,0:T(8,128)S(1)}, bf16[8,64,256]{2,1,0:T(8,128)(2,1)S(1)}, bf16[272,256]{1,0:T(8,128)(2,1)S(1)}, bf16[8,64,128]{2,1,0:T(8,128)(2,1)S...) custom-call(s32[32]{0:T(128)} %live_hbm.1, bf16[64,2048]{1,0:T(8,128)(2,1)} %y_hbm.1, ...), custom_call_target="tpu_custom_call" | custom-call | tf_op jit(solution)/shard_map/exchange/pallas_call | solution.py:486
  22.4 1.2 %update.1 = (f32[64,256]{1,0:T(8,128)}, bf16[272,256]{1,0:T(8,128)(2,1)}) custom-call(f32[64,256]{1,0:T(8,128)S(1)} %get-tuple-element.9.tr, bf16[8,64,256]{2,1,0:T(8,128)(2,1)S(1)} %get-tuple-element.10.b_all, bf16[272,256]{1,0:T(8,128)(2,1)S(1)} %get-tuple-element.11.yt, bf16[8,64,128]{2,1,0:T(8,128)(2,1)S(1)} %get-tuple-element.12.side, ...), custom_call_target="tpu_custom_call" | custom-call | tf_op jit(solution)/shard_map/update/pallas_call | solution.py:530

commit v9 on v7

--- a/solution.py
+++ b/solution.py
@@ -210,6 +210,11 @@
     own_drive = dot(yv[...], av[:voxels])
     coupled = dot(start, gram, precision=lax.Precision.HIGHEST)
     base = own_drive - coupled
+    between = {}
+    for g in range(neurons // GROUP):
+        for h in range(g):
+            g_high, g_low = halves(gram[h * GROUP : (h + 1) * GROUP, g * GROUP : (g + 1) * GROUP])
+            between[h, g] = jnp.concatenate([g_high, g_high, g_low], 0)
 
     @pl.when(has_next)
     def _():
@@ -238,15 +243,10 @@
         cut = slice(g * GROUP, (g + 1) * GROUP)
         change = base[:, cut]
         for h in range(g):
-            moved = done[h] - start[:, h * GROUP : (h + 1) * GROUP]
-            change = change - dot(
-                moved, gram[h * GROUP : (h + 1) * GROUP, cut], precision=lax.Precision.HIGHEST
-            )
-        done.append(
-            jnp.where(
-                live[:, cut], jnp.maximum(start[:, cut] + change / scale[:, cut], 0.0), 0.0
-            )
-        )
+            m_high, m_low = halves(done[h] - start[:, h * GROUP : (h + 1) * GROUP])
+            change = change - dot(jnp.concatenate([m_high, m_low, m_high], 1), between[h, g])
+        moved = jnp.maximum(start[:, cut] + change / scale[:, cut], 0.0)
+        done.append(jnp.where(live[:, cut], moved, 0.0))
     new_tr = jnp.concatenate(done, 1)
     rounded = new_tr.astype(BF16)
     b_all[0] = rounded

time: 23.7 us -> 23.8 us (level)
  no operation moved by 1% of the time
where the time goes in v9:
time: 23.8 us; the launch traced here: 23.7 us
  Pallas kernels  23 us (97%)
  between operations  0.64 us (3%)
    pallas_call x1, Pallas kernels, on_device(): pl.pallas_call(functools.partial(exchange_kernel, dims), out_shape=[pltpu...  21.9 us
    pallas_call x1, Pallas kernels, on_device(): pl.pallas_call(functools.partial(update_kernel, dims), out_shape=[jax.Sha...  1.15 us

profile of v9, /device:TPU:32, one launch (start us, length us, event | category | flops | bytes accessed | tf_op | source)
XLA Modules:
  0.0 23.7 jit_solution(6489814657616349488)
XLA Ops:
  0.6 21.9 %exchange.1 = (f32[64,256]{1,0:T(8,128)S(1)}, bf16[8,64,256]{2,1,0:T(8,128)(2,1)S(1)}, bf16[272,256]{1,0:T(8,128)(2,1)S(1)}, bf16[8,64,128]{2,1,0:T(8,128)(2,1)S...) custom-call(s32[32]{0:T(128)} %live_hbm.1, bf16[64,2048]{1,0:T(8,128)(2,1)} %y_hbm.1, ...), custom_call_target="tpu_custom_call" | custom-call | tf_op jit(solution)/shard_map/exchange/pallas_call | solution.py:486
  22.5 1.2 %update.1 = (f32[64,256]{1,0:T(8,128)}, bf16[272,256]{1,0:T(8,128)(2,1)}) custom-call(f32[64,256]{1,0:T(8,128)S(1)} %get-tuple-element.9.tr, bf16[8,64,256]{2,1,0:T(8,128)(2,1)S(1)} %get-tuple-element.10.b_all, bf16[272,256]{1,0:T(8,128)(2,1)S(1)} %get-tuple-element.11.yt, bf16[8,64,128]{2,1,0:T(8,128)(2,1)S(1)} %get-tuple-element.12.side, ...), custom_call_target="tpu_custom_call" | custom-call | tf_op jit(solution)/shard_map/update/pallas_call | solution.py:530

commit v10 on v9

--- a/solution.py
+++ b/solution.py
@@ -189,7 +189,7 @@
                 due = jnp.int32(LATE_CROSS[0][i - half])
                 for zone, stages in enumerate(LATE_CROSS):
                     due = jnp.where(s * len(LATE_CROSS) // slabs == zone, stages[i - half], due)
-                due = jnp.where(late, jnp.where(to == 0, 0, due), EARLY_CROSS)
+                due = jnp.where(late, jnp.where((to == 0) & (s * len(LATE_CROSS) // slabs > 0), 0, due), EARLY_CROSS)
             else:
                 due = jnp.where(patient, 3, jnp.where(late, 2, 0))
             due = jnp.where(to == parts - 1, jnp.maximum(due, 2), due)

time: 23.8 us -> 23.8 us (level)
  no operation moved by 1% of the time
where the time goes in v10:
time: 23.8 us; the launch traced here: 23.7 us
  Pallas kernels  23 us (97%)
  between operations  0.64 us (3%)
    pallas_call x1, Pallas kernels, on_device(): pl.pallas_call(functools.partial(exchange_kernel, dims), out_shape=[pltpu...  21.9 us
    pallas_call x1, Pallas kernels, on_device(): pl.pallas_call(functools.partial(update_kernel, dims), out_shape=[jax.Sha...  1.15 us

profile of v10, /device:TPU:32, one launch (start us, length us, event | category | flops | bytes accessed | tf_op | source)
XLA Modules:
  0.0 23.7 jit_solution(4861866094145557212)
XLA Ops:
  0.6 21.9 %exchange.1 = (f32[64,256]{1,0:T(8,128)S(1)}, bf16[8,64,256]{2,1,0:T(8,128)(2,1)S(1)}, bf16[272,256]{1,0:T(8,128)(2,1)S(1)}, bf16[8,64,128]{2,1,0:T(8,128)(2,1)S...) custom-call(s32[32]{0:T(128)} %live_hbm.1, bf16[64,2048]{1,0:T(8,128)(2,1)} %y_hbm.1, ...), custom_call_target="tpu_custom_call" | custom-call | tf_op jit(solution)/shard_map/exchange/pallas_call | solution.py:486
  22.5 1.2 %update.1 = (f32[64,256]{1,0:T(8,128)}, bf16[272,256]{1,0:T(8,128)(2,1)}) custom-call(f32[64,256]{1,0:T(8,128)S(1)} %get-tuple-element.9.tr, bf16[8,64,256]{2,1,0:T(8,128)(2,1)S(1)} %get-tuple-element.10.b_all, bf16[272,256]{1,0:T(8,128)(2,1)S(1)} %get-tuple-element.11.yt, bf16[8,64,128]{2,1,0:T(8,128)(2,1)S(1)} %get-tuple-element.12.side, ...), custom_call_target="tpu_custom_call" | custom-call | tf_op jit(solution)/shard_map/update/pallas_call | solution.py:530
